TPU v7x, 32 devices: a whole 2x2x4 slice. The times are simulated.
32 devices in a mesh: key: 8 (over z, x), lvl: 4 (over y, core).
Axes of the slice: x: 2, y: 2, z: 4, core: 2. Of those that a mesh axis runs over, the one named last changes fastest.
Arguments:
- multipoles: bfloat16 [1024, 4096], P(('key', 'lvl')), may hold values from -6 to 6
- operators: bfloat16 [189, 64, 64], replicated, may hold values from -0.0546875 to 0.0546875
- pair_source: int32 [1024, 189], P(('key', 'lvl')), may hold values from 0 to 1087, as said below
- pair_offset: int32 [1024, 189], P(('key', 'lvl')), may hold values from 0 to 188, each once within a row
- live_pairs: int32 [1024], P(('key', 'lvl')), may hold values from 1 to 189
- send_lists: int32 [32, 32, 2], replicated, may hold values from 0 to 1023, as said below
- occupied: int32 [1024, 64], P(('key', 'lvl')), may hold values 0 or 1
Outputs:
- locals_out: float32 [1024, 4096], P(('key', 'lvl'))
Inputs may be any that keep to these rules, and one draw needn't show every extreme that they name: `pair_source`: batch b belongs to device b // 32 (device index over key+lvl, key slowest). A value below 1024 is a batch of device j - 1, j or j + 1 for a target on device j. send_lists[i, j, k] is a batch owned by device i.
All inputs are finite; a program needn't handle non-finite values. No bound on the sum of `occupied` on one device may be relied on, other than what follows from the above.
Results may differ from a plain program's by a relative error of at most 0.0003.
Values may be sent and summed in bfloat16 or wider, within the bound.
No kernel may reach another device: no remote copies, remote signals or barrier semaphores. Data moves between devices by JAX's collectives and lax.ppermute only.
A program may use at most 64 MiB of HBM per device.

v0:
```python
import functools

import jax
import jax.numpy as jnp
from jax import lax
from jax.experimental import pallas as pl
from jax.experimental.pallas import tpu as pltpu
from jax.sharding import PartitionSpec as P

F32 = jnp.float32
BF16 = jnp.bfloat16
I32 = jnp.int32
VMEM = pl.BlockSpec(memory_space=pltpu.VMEM)
SMEM = pl.BlockSpec(memory_space=pltpu.SMEM)
GROUP = 8
FEW = 8
ITEMS = 8
LANES = 128
NT = (((1,), (1,)), ((), ()))


def params(mib):
    return pltpu.CompilerParams(vmem_limit_bytes=mib << 20)


def padded(n, m):
    return -(-n // m) * m


def pack_kernel(me, send, m_hbm, own, outgoing, m, ids, scr, sems):
    batches, pairs = own.shape[0], own.shape[1]
    slots, devices = ids.shape
    rows = pltpu.make_async_copy(m_hbm, m, sems.at[0])
    lists = pltpu.make_async_copy(send.at[me[0]], ids, sems.at[1])
    rows.start()
    lists.start()
    rows.wait()
    for i in range(pairs):
        for h in range(0, batches, 16):
            x = m[h : h + 16, i * LANES : (i + 1) * LANES].astype(F32)
            scr[pl.ds(h * pairs + i, 16, stride=pairs), :] = x
    for b in range(batches):
        own[b] = scr[b * pairs : (b + 1) * pairs, :].astype(BF16)
    lists.wait()
    first = me[0] * batches

    def send_to(j, _):
        for k in range(slots):
            outgoing[j * slots + k] = own[ids[k, j] - first]
        return 0

    lax.fori_loop(0, devices, send_to, 0, unroll=8)


def ops_kernel(native, twice, scr):
    coeffs, offsets = native.shape[0], native.shape[2]
    half = coeffs // 2
    low = lax.broadcasted_iota(I32, (half, LANES), 1) < coeffs
    for i in range(half):
        x = jnp.concatenate([native[i], native[half + i]], axis=0).astype(F32)
        scr[pl.ds(i, offsets, stride=half), :] = x.T

    def spread(l, _):
        x = scr[pl.ds(pl.multiple_of(l * half, half), half), :]
        y = pltpu.roll(x, coeffs, 1)
        twice[l, 0:half] = jnp.where(low, x, y).astype(BF16)
        twice[l, half:coeffs] = jnp.where(low, y, x).astype(BF16)
        return 0

    lax.fori_loop(0, offsets, spread, 0, unroll=7)


def table_kernel(total_batches, base, src, off, live, near_tbl, far_slot, far_off, far_items):
    rows, lst = src.shape
    wide = near_tbl.shape[1]
    s = src[...]
    o = off[...]
    mine = base[0]
    twin = base[1]
    other = base[2]
    at_r = lax.broadcasted_iota(I32, (rows, rows), 0)
    at_c = lax.broadcasted_iota(I32, (rows, rows), 1)
    count_col = jnp.sum(jnp.where(at_r == at_c, live[...], 0), axis=1, keepdims=True)
    col = lax.broadcasted_iota(I32, (rows, lst), 1)
    alive = col < count_col
    far = s >= total_batches
    in_mine = (s >= mine) & (s < mine + rows)
    in_twin = (s >= twin) & (s < twin + rows)
    place = jnp.where(in_mine, s - mine, jnp.where(in_twin, s - twin + rows, s - other + 2 * rows))
    near_val = jnp.where(alive & jnp.logical_not(far), place + 1, 0)
    far_live = alive & far
    far_val = jnp.where(far_live, s - total_batches + 1, 0)
    one = jnp.where(far_live, 1.0, 0.0)
    before = lax.broadcasted_iota(I32, (lst, lst), 0) < lax.broadcasted_iota(I32, (lst, lst), 1)
    rank = jnp.dot(one.astype(BF16), jnp.where(before, 1.0, 0.0).astype(BF16), preferred_element_type=F32)
    pos = jnp.where(far_live, rank.astype(I32), wide)
    count = jnp.sum(one, axis=1, keepdims=True).astype(I32)
    items = jnp.maximum((count + (FEW - 1)) // FEW, 1)
    far_items[...] = jnp.ones_like(far_items)
    far_items[0:rows, :] = jnp.broadcast_to(items, (rows, LANES))
    near_b = near_val.astype(F32).astype(BF16)
    far_b = jnp.concatenate([far_val & 127, far_val >> 7, o], axis=0).astype(F32).astype(BF16)
    want = lax.broadcasted_iota(I32, (wide, lst), 0)
    far_slot[...] = jnp.zeros_like(far_slot)
    far_off[...] = jnp.zeros_like(far_off)
    for t in range(rows):
        hot = jnp.where(want == o[t : t + 1, :], 1.0, 0.0).astype(BF16)
        got = lax.dot_general(near_b, hot, NT, preferred_element_type=F32)
        near_tbl[t : t + 1, :] = got[t : t + 1, :].astype(I32)
        hot = jnp.where(want == pos[t : t + 1, :], 1.0, 0.0).astype(BF16)
        got = lax.dot_general(far_b, hot, NT, preferred_element_type=F32).astype(I32)
        far_slot[t : t + 1, :] = got[t : t + 1, :] + 128 * got[rows + t : rows + t + 1, :]
        far_off[t : t + 1, :] = got[2 * rows + t : 2 * rows + t + 1, :]


def near_kernel(tbl, own, twin, other, ops, acc, pool):
    batches = own.shape[0]
    last = ops.shape[0] - 1
    zero = jnp.zeros(pool.shape[1:], BF16)
    pool[0] = zero
    for n, part in enumerate((own, twin, other)):
        for b in range(batches):
            pool[1 + n * batches + b] = part[b]
    acc[...] = jnp.zeros_like(acc)
    blank = jnp.zeros(ops.shape[1:], BF16)
    low = lax.broadcasted_iota(I32, blank.shape, 1) < blank.shape[0]

    def group(g, _):
        blocks = []
        for h in range(GROUP):
            op = ops[jnp.minimum(g * GROUP + h, last)]
            blocks.append(jnp.concatenate([jnp.where(low, op, blank), jnp.where(low, blank, op)], axis=0))
        w = jnp.concatenate(blocks, axis=1)
        rows = []
        for t in range(batches):
            rows.append(jnp.concatenate([pool[tbl[t, g * GROUP + h]] for h in range(GROUP)], axis=1))
        x = jnp.concatenate(rows, axis=0)
        acc[...] += lax.dot_general(x, w, NT, preferred_element_type=F32).reshape(acc.shape)
        return 0

    lax.fori_loop(0, tbl.shape[1] // GROUP, group, 0)


def far_kernel(slots, offs, items, arrived, ops, near, occ, out, pool, acc):
    batches, pairs = near.shape[0], near.shape[1]
    half = ops.shape[1]
    pool[0] = jnp.zeros(pool.shape[1:], BF16)

    def fill(n, _):
        x = arrived[n]
        pool[n + 1, 0:pairs] = x
        pool[n + 1, pairs : 2 * pairs] = jnp.concatenate([x[:, half:], x[:, :half]], axis=1)
        return 0

    lax.fori_loop(0, arrived.shape[0], fill, 0, unroll=8)
    acc[0 : batches * pairs, :] = near[...].reshape(batches * pairs, LANES)
    acc[batches * pairs :, :] = jnp.zeros((pairs, LANES), F32)
    low = lax.broadcasted_iota(I32, (pairs, LANES), 1) < half
    low_op = lax.broadcasted_iota(I32, (half, LANES), 1) < half
    total = lax.fori_loop(0, batches, lambda t, n: n + items[t, 0], 0)

    def step(i, place):
        t, g = place
        for u in range(ITEMS):
            xs, ws = [], []
            for h in range(0, FEW, 2):
                e = g * FEW + h
                a, b = slots[t, e], slots[t, e + 1]
                even = jnp.where(low, pool[a, 0:pairs], pool[b, pairs : 2 * pairs])
                odd = jnp.where(low, pool[a, pairs : 2 * pairs], pool[b, 0:pairs])
                xs.append(jnp.concatenate([even, odd], axis=0))
                ws.append(jnp.where(low_op, ops[offs[t, e]], ops[offs[t, e + 1]]))
            r = lax.dot_general(jnp.concatenate(xs, axis=1), jnp.concatenate(ws, axis=1), NT, preferred_element_type=F32)
            at = pl.ds(pl.multiple_of(t * pairs, pairs), pairs)
            acc[at, :] += jnp.concatenate([r[:pairs], r[pairs:]], axis=1)
            end = g + 1 >= items[t, 0]
            t = jnp.where(end, jnp.minimum(t + 1, batches), t)
            g = jnp.where(end, 0, g + 1)
        return t, g

    lax.fori_loop(0, (total + (ITEMS - 1)) // ITEMS, step, (jnp.int32(0), jnp.int32(0)))
    cells = occ.shape[1]
    filled = occ[...].astype(F32).astype(BF16)
    cell = lax.broadcasted_iota(I32, (cells, LANES), 0)
    upper = (lax.broadcasted_iota(I32, (cells, LANES), 1) >= half).astype(I32)
    for i in range(pairs):
        spread = jnp.where(cell == upper + 2 * i, 1.0, 0.0).astype(BF16)
        keep = jnp.dot(filled, spread, preferred_element_type=F32)
        out[:, i * LANES : (i + 1) * LANES] = acc[pl.ds(i, batches, stride=pairs), :] * keep


def local(multipoles, operators, pair_source, pair_offset, live_pairs, send_lists, occupied):
    axes = ("key", "lvl")
    batches, width = multipoles.shape
    offsets, coeffs = operators.shape[0], operators.shape[1]
    devices = lax.axis_size(axes)
    slots = send_lists.shape[2]
    me = lax.axis_index(axes)
    pairs = width // LANES
    wide = padded(offsets, GROUP)
    wide = padded(wide, 64)
    block = (pairs, LANES)

    any_space = pl.BlockSpec(memory_space=pl.ANY)
    own, outgoing = pl.pallas_call(
        pack_kernel,
        out_shape=(
            jax.ShapeDtypeStruct((batches,) + block, BF16),
            jax.ShapeDtypeStruct((devices * slots,) + block, BF16),
        ),
        in_specs=[SMEM, any_space, any_space],
        out_specs=(VMEM, VMEM),
        scratch_shapes=[
            pltpu.VMEM((batches, width), BF16),
            pltpu.SMEM((slots, devices), I32),
            pltpu.VMEM((batches * pairs, LANES), F32),
            pltpu.SemaphoreType.DMA((2,)),
        ],
        compiler_params=params(16),
        name="pack",
    )(me.reshape(1), send_lists.transpose(0, 2, 1), multipoles)
    even = [(i, i ^ 1) for i in range(devices)]
    odd = [p for i in range(1, devices - 1, 2) for p in ((i, i + 1), (i + 1, i))]
    arrived = lax.all_to_all(outgoing, axes, split_axis=0, concat_axis=0, tiled=True)
    twin = lax.ppermute(own, axes, even)
    other = lax.ppermute(own, axes, odd)
    first = jnp.stack([me, me ^ 1, me - 1 + 2 * (me & 1)]) * batches

    tall = padded(batches + 1, 8)
    near_tbl, far_slot, far_off, far_items = pl.pallas_call(
        functools.partial(table_kernel, batches * devices),
        out_shape=(
            jax.ShapeDtypeStruct((batches, wide), I32),
            jax.ShapeDtypeStruct((tall, wide), I32),
            jax.ShapeDtypeStruct((tall, wide), I32),
            jax.ShapeDtypeStruct((tall, LANES), I32),
        ),
        in_specs=[SMEM, VMEM, VMEM, VMEM],
        out_specs=(VMEM,) * 4,
        compiler_params=params(16),
        name="tables",
    )(first, pair_source, pair_offset, live_pairs.reshape(1, batches))

    ops = pl.pallas_call(
        ops_kernel,
        out_shape=jax.ShapeDtypeStruct((offsets, coeffs, LANES), BF16),
        in_specs=[VMEM],
        out_specs=VMEM,
        scratch_shapes=[pltpu.VMEM((offsets * coeffs // 2, LANES), F32)],
        compiler_params=params(24),
        name="ops",
    )(operators.transpose(1, 2, 0))
    near = pl.pallas_call(
        near_kernel,
        out_shape=jax.ShapeDtypeStruct((batches,) + block, F32),
        in_specs=[SMEM] + [VMEM] * 4,
        out_specs=VMEM,
        scratch_shapes=[pltpu.VMEM((3 * batches + 1,) + block, BF16)],
        compiler_params=params(24),
        cost_estimate=pl.CostEstimate(flops=12_000_000_000, bytes_accessed=4_000_000, transcendentals=0),
        name="near",
    )(near_tbl, own, twin, other, ops)

    return pl.pallas_call(
        far_kernel,
        out_shape=jax.ShapeDtypeStruct((batches, width), F32),
        in_specs=[SMEM] * 3 + [VMEM] * 4,
        out_specs=VMEM,
        scratch_shapes=[
            pltpu.VMEM((devices * slots + 1, 2 * pairs, LANES), BF16),
            pltpu.VMEM(((batches + 1) * pairs, LANES), F32),
        ],
        compiler_params=params(32),
        name="far",
    )(far_slot, far_off, far_items, arrived, ops, near, occupied)


def solution(mesh):
    spec = P(("key", "lvl"), None)
    return jax.shard_map(
        local,
        mesh=mesh,
        in_specs=(spec, P(), spec, spec, P(("key", "lvl")), P(), spec),
        out_specs=spec,
        check_vma=False,
    )
```

profile of v0, /device:TPU:1, one launch (start us, length us, event | category | flops | bytes accessed | tf_op | source)
XLA Modules:
  0.0 50.1 jit_solution(5584330959335573476)
XLA Ops:
  0.0 0.0 copy-start.3
  0.0 0.9 %copy-done.3 = bf16[32,4096]{1,0:T(8,128)(2,1)S(1)} copy-done((bf16[32,4096]{1,0:T(8,128)(2,1)S(1)}, bf16[32,4096]{1,0:T(8,128)(2,1)}, u32[]{:S(2)}) %copy-start.3) | copy-done | bytes 262168
  1.0 0.0 copy-start.4
  1.0 0.8 %copy-done.4 = s32[32,32,2]{1,2,0:T(2,128)S(1)} copy-done((s32[32,32,2]{1,2,0:T(2,128)S(1)}, s32[32,32,2]{1,2,0:T(2,128)}, u32[]{:S(2)}) %copy-start.4) | copy-done | bytes 8216
  1.7 1.5 %pack.1 = (bf16[32,32,128]{2,1,0:T(8,128)(2,1)S(1)}, bf16[64,32,128]{2,1,0:T(8,128)(2,1)}) custom-call(s32[1]{0:T(128)} %bitcast.me, s32[32,2,32]{2,1,0:T(2,128)S(1)} %bitcast.7, bf16[32,4096]{1,0:T(8,128)(2,1)S(1)} %copy-done.3), custom_call_target="tpu_custom_call" | custom-call | tf_op jit(solution)/shard_map/pack/pallas_call | solution.py:205
  3.2 4.5 %collective-permute-start.1 = (bf16[32,32,128]{2,1,0:T(8,128)(2,1)S(1)}, bf16[32,32,128]{2,1,0:T(8,128)(2,1)}, u32[]{:S(2)}, u32[]{:S(2)}) collective-permute-start(bf16[32,32,128]{2,1,0:T(8,128)(2,1)S(1)} %get-tuple-element.16.own), channel_id=1, source_target_pairs={{1,2},{2,1},{3,4},{4,3},{5,6},{6,5},{7,8},{8,7},{9,10},{10,9},{11,... | collective-permute-start | bytes 786440 | tf_op jit(solution)/shard_map/ppermute | solution.py:226
  7.8 0.1 collective-permute-start
  7.9 0.0 copy-start.5
  7.9 0.0 copy-start.6
  7.9 0.0 copy-start.8
  7.9 5.2 %all-to-all-start = ((bf16[64,32,128]{2,1,0:T(8,128)(2,1)}), bf16[64,32,128]{2,1,0:T(8,128)(2,1)}, u32[]{:S(2)}, u32[]{:S(2)}) async-start(bf16[64,32,128]{2,1,0:T(8,128)(2,1)} %get-tuple-element.14), calls=%async_computation | async-start | bytes 1048576 | tf_op jit(solution)/shard_map/all_to_all | solution.py:224
  13.1 0.0 copy-start
  13.1 1.6 %copy-done = bf16[189,64,64]{0,2,1:T(8,128)(2,1)S(1)} copy-done((bf16[189,64,64]{0,2,1:T(8,128)(2,1)S(1)}, bf16[189,64,64]{0,2,1:T(8,128)(2,1)}, u32[]{:S(2)}) %copy-start) | copy-done | bytes 1548312
  14.7 4.5 %ops.1 = bf16[189,64,128]{2,1,0:T(8,128)(2,1)S(1)} custom-call(bf16[64,64,189]{2,1,0:T(8,128)(2,1)S(1)} %bitcast.6), custom_call_target="tpu_custom_call" | custom-call | tf_op jit(solution)/shard_map/ops/pallas_call | solution.py:244
  19.1 0.1 add_multiply_fusion.base
  19.2 0.0 copy-done.5
  19.2 0.0 copy-done.6
  19.2 0.0 copy-done.8
  19.2 2.5 %tables.1 = (s32[32,192]{1,0:T(8,128)S(1)}, s32[40,192]{1,0:T(8,128)S(1)}, s32[40,192]{1,0:T(8,128)S(1)}, s32[40,128]{1,0:T(8,128)S(1)}) custom-call(s32[3]{0:T(128)S(1)} %add_multiply_fusion.base, s32[32,189]{1,0:T(8,128)S(1)} %copy-done.5, s32[32,189]{1,0:T(8,128)S(1)} %copy-done.6, s32[1,32]{1,0:T(1,128)S(1)} %bitcast.8), custom_call_target="tpu_custom_call" | custom-call | tf_op jit(solution)/shard_map/tables/pallas_call | solution.py:230
  21.8 0.0 collective-permute-done.1.other
  21.8 0.0 collective-permute-done.twin
  21.8 0.0 copy-start.7
  21.8 18.7 %near.1 = f32[32,32,128]{2,1,0:T(8,128)S(1)} custom-call(s32[32,192]{1,0:T(8,128)S(1)} %get-tuple-element.15.tbl, bf16[32,32,128]{2,1,0:T(8,128)(2,1)S(1)} %get-tuple-element.16.own, bf16[32,32,128]{2,1,0:T(8,128)(2,1)} %collective-permute-done.twin, bf16[32,32,128]{2,1,0:T(8,128)(2,1)} %collective-permute-done.1.other, bf16[189,64,128]{2,1,0:T(8,128)(2,1)S(1)} %ops.1), custom_call_target="tpu_custom_call" | custom-call | flops 12000000000 | bytes 4000000 | tf_op jit(solution)/shard_map/near/pallas_call | solution.py:253
  40.5 0.0 copy-start.1
  40.5 0.8 %copy-done.1 = f32[32,32,128]{2,1,0:T(8,128)} copy-done((f32[32,32,128]{2,1,0:T(8,128)}, f32[32,32,128]{2,1,0:T(8,128)S(1)}, u32[]{:S(2)}) %copy-start.1) | copy-done | bytes 524312
  41.3 0.0 all-to-all-done.arrived
  41.3 0.0 copy-done.7
  41.3 0.0 copy-start.2
  41.3 1.0 %copy-done.2 = f32[32,32,128]{2,1,0:T(8,128)S(1)} copy-done((f32[32,32,128]{2,1,0:T(8,128)S(1)}, f32[32,32,128]{2,1,0:T(8,128)}, u32[]{:S(2)}) %copy-start.2) | copy-done | bytes 524312
  42.4 7.7 %far.1 = f32[32,4096]{1,0:T(8,128)} custom-call(s32[40,192]{1,0:T(8,128)S(1)} %get-tuple-element.11.slots, s32[40,192]{1,0:T(8,128)S(1)} %get-tuple-element.12.offs, s32[40,128]{1,0:T(8,128)S(1)} %get-tuple-element.13.items, bf16[64,32,128]{2,1,0:T(8,128)(2,1)} %all-to-all-done.arrived, bf16[189,64,128]{2,1,0:T(8,128)(2,1)S(1)} %ops.1, ...), custom_call_target="tpu_custom_call" | custom-call | tf_op jit(solution)/shard_map/far/pallas_call | solution.py:264
Async XLA Ops:
  0.0 0.9 %copy-start.3 = (bf16[32,4096]{1,0:T(8,128)(2,1)S(1)}, bf16[32,4096]{1,0:T(8,128)(2,1)}, u32[]{:S(2)}) copy-start(bf16[32,4096]{1,0:T(8,128)(2,1)} %m_hbm.1) | copy-start | bytes 786436
  1.0 0.8 %copy-start.4 = (s32[32,32,2]{1,2,0:T(2,128)S(1)}, s32[32,32,2]{1,2,0:T(2,128)}, u32[]{:S(2)}) copy-start(s32[32,32,2]{1,2,0:T(2,128)} %param.12) | copy-start | bytes 24580
  3.2 18.5 %collective-permute-start.1 = (bf16[32,32,128]{2,1,0:T(8,128)(2,1)S(1)}, bf16[32,32,128]{2,1,0:T(8,128)(2,1)}, u32[]{:S(2)}, u32[]{:S(2)}) collective-permute-start(bf16[32,32,128]{2,1,0:T(8,128)(2,1)S(1)} %get-tuple-element.16.own), channel_id=1, source_target_pairs={{1,2},{2,1},{3,4},{4,3},{5,6},{6,5},{7,8},{8,7},{9,10},{10,9},{11,... | collective-permute-start | bytes 786440 | tf_op jit(solution)/shard_map/ppermute | solution.py:226
  7.8 14.0 %collective-permute-start = (bf16[32,32,128]{2,1,0:T(8,128)(2,1)S(1)}, bf16[32,32,128]{2,1,0:T(8,128)(2,1)}, u32[]{:S(2)}, u32[]{:S(2)}) collective-permute-start(bf16[32,32,128]{2,1,0:T(8,128)(2,1)S(1)} %get-tuple-element.16.own), channel_id=1, source_target_pairs={{0,1},{1,0},{2,3},{3,2},{4,5},{5,4},{6,7},{7,6},{8,9},{9,8},{10,11... | collective-permute-start | bytes 786440 | tf_op jit(solution)/shard_map/ppermute | solution.py:225
  7.9 11.3 %copy-start.5 = (s32[32,189]{1,0:T(8,128)S(1)}, s32[32,189]{1,0:T(8,128)}, u32[]{:S(2)}) copy-start(s32[32,189]{1,0:T(8,128)} %src.1) | copy-start | bytes 72580
  7.9 11.3 %copy-start.6 = (s32[32,189]{1,0:T(8,128)S(1)}, s32[32,189]{1,0:T(8,128)}, u32[]{:S(2)}) copy-start(s32[32,189]{1,0:T(8,128)} %off.1) | copy-start | bytes 72580
  7.9 11.3 %copy-start.8 = (s32[32]{0:T(128)S(1)}, s32[32]{0:T(128)}, u32[]{:S(2)}) copy-start(s32[32]{0:T(128)} %param.11) | copy-start | bytes 388
  7.9 33.4 %all-to-all-start = ((bf16[64,32,128]{2,1,0:T(8,128)(2,1)}), bf16[64,32,128]{2,1,0:T(8,128)(2,1)}, u32[]{:S(2)}, u32[]{:S(2)}) async-start(bf16[64,32,128]{2,1,0:T(8,128)(2,1)} %get-tuple-element.14), calls=%async_computation | async-start | bytes 1048576 | tf_op jit(solution)/shard_map/all_to_all | solution.py:224
  13.1 1.6 %copy-start = (bf16[189,64,64]{0,2,1:T(8,128)(2,1)S(1)}, bf16[189,64,64]{0,2,1:T(8,128)(2,1)}, u32[]{:S(2)}) copy-start(bf16[189,64,64]{0,2,1:T(8,128)(2,1)} %param.8) | copy-start | bytes 4644868
  21.8 19.6 %copy-start.7 = (s32[32,64]{1,0:T(8,128)S(1)}, s32[32,64]{1,0:T(8,128)}, u32[]{:S(2)}) copy-start(s32[32,64]{1,0:T(8,128)} %occ.1) | copy-start | bytes 24580
  40.5 0.8 %copy-start.1 = (f32[32,32,128]{2,1,0:T(8,128)}, f32[32,32,128]{2,1,0:T(8,128)S(1)}, u32[]{:S(2)}) copy-start(f32[32,32,128]{2,1,0:T(8,128)S(1)} %near.1) | copy-start | bytes 1572868
  41.3 1.0 %copy-start.2 = (f32[32,32,128]{2,1,0:T(8,128)S(1)}, f32[32,32,128]{2,1,0:T(8,128)}, u32[]{:S(2)}) copy-start(f32[32,32,128]{2,1,0:T(8,128)} %copy-done.1) | copy-start | bytes 1572868
where the time goes:
time: 50.9 us; the launch traced here: 50.1 us
  Pallas kernels  34.9 us (69%)
  starting transfers between devices  9.77 us (19%)
  local copies, waits for them, and re-layouts  5.16 us (10%)
    pallas_call x1, Pallas kernels, local(): pl.pallas_call(near_kernel, out_shape=jax.ShapeDtypeStruct((batches,) + b...  18.7 us
    pallas_call x1, Pallas kernels, local(): pl.pallas_call(far_kernel, out_shape=jax.ShapeDtypeStruct((batches, width...  7.7 us
    unnamed x18, local copies, waits for them, and re-layouts  5.16 us
    all_to_all x1, starting transfers between devices, local(): lax.all_to_all(outgoing, axes, split_axis=0, concat_axis=0, tiled=True)  5.16 us
    ppermute x1, starting transfers between devices, local(): other = lax.ppermute(own, axes, odd)  4.54 us
    pallas_call x1, Pallas kernels, local(): pl.pallas_call(ops_kernel, out_shape=jax.ShapeDtypeStruct((offsets, coeff...  4.45 us
    pallas_call x1, Pallas kernels, local(): pl.pallas_call(functools.partial(table_kernel, batches * devices), out_sh...  2.54 us
    pallas_call x1, Pallas kernels, local(): pl.pallas_call(pack_kernel, out_shape=(jax.ShapeDtypeStruct((batches,) +...  1.51 us
  transfers between devices with their start and end apart: 3, of which 0 were waited for; matrix products, arithmetic and copies ran while one was open for 0% of the time, Pallas kernels for 51%

commit v1 on v0

--- a/solution.py
+++ b/solution.py
@@ -12,9 +12,10 @@
 I32 = jnp.int32
 VMEM = pl.BlockSpec(memory_space=pltpu.VMEM)
 SMEM = pl.BlockSpec(memory_space=pltpu.SMEM)
-GROUP = 8
+HBM = pl.BlockSpec(memory_space=pltpu.HBM)
+GROUP = 16
 FEW = 8
-ITEMS = 8
+ITEMS = 16
 LANES = 128
 NT = (((1,), (1,)), ((), ()))
 
@@ -52,13 +53,18 @@
     lax.fori_loop(0, devices, send_to, 0, unroll=8)
 
 
-def ops_kernel(native, twice, scr):
+def spread_ops(native, twice, scr):
     coeffs, offsets = native.shape[0], native.shape[2]
     half = coeffs // 2
+    tall = twice.shape[0]
+    at = lax.broadcasted_iota(I32, (tall, offsets), 0)
+    eye = jnp.where(at == lax.broadcasted_iota(I32, (tall, offsets), 1), 1.0, 0.0).astype(BF16)
+    for i in range(0, half, 2):
+        x = jnp.concatenate([native[i], native[half + i], native[i + 1], native[half + i + 1]], axis=0)
+        y = lax.dot_general(eye, x, NT, preferred_element_type=F32)
+        scr[pl.ds(i, tall, stride=half), :] = y[:, :LANES]
+        scr[pl.ds(i + 1, tall, stride=half), :] = y[:, LANES:]
     low = lax.broadcasted_iota(I32, (half, LANES), 1) < coeffs
-    for i in range(half):
-        x = jnp.concatenate([native[i], native[half + i]], axis=0).astype(F32)
-        scr[pl.ds(i, offsets, stride=half), :] = x.T
 
     def spread(l, _):
         x = scr[pl.ds(pl.multiple_of(l * half, half), half), :]
@@ -67,10 +73,10 @@
         twice[l, half:coeffs] = jnp.where(low, y, x).astype(BF16)
         return 0
 
-    lax.fori_loop(0, offsets, spread, 0, unroll=7)
-
-
-def table_kernel(total_batches, base, src, off, live, near_tbl, far_slot, far_off, far_items):
+    lax.fori_loop(0, tall, spread, 0, unroll=8)
+
+
+def make_tables(total_batches, base, src, off, live, near_tbl, far_slot, far_off, far_items):
     rows, lst = src.shape
     wide = near_tbl.shape[1]
     s = src[...]
@@ -113,22 +119,32 @@
         far_off[t : t + 1, :] = got[2 * rows + t : 2 * rows + t + 1, :]
 
 
-def near_kernel(tbl, own, twin, other, ops, acc, pool):
+def near_kernel(
+    total_batches, base, src, off, live, native_hbm, own, twin, other,
+    sums, ops, far_slot, far_off, far_items,
+    native, scr, tbl_v, tbl, pool, acc, sems,
+):
+    fetch = pltpu.make_async_copy(native_hbm, native, sems.at[0])
+    fetch.start()
+    make_tables(total_batches, base, src, off, live, tbl_v, far_slot, far_off, far_items)
+    to_smem = pltpu.make_async_copy(tbl_v, tbl, sems.at[1])
+    to_smem.start()
     batches = own.shape[0]
-    last = ops.shape[0] - 1
-    zero = jnp.zeros(pool.shape[1:], BF16)
-    pool[0] = zero
+    pool[0] = jnp.zeros(pool.shape[1:], BF16)
     for n, part in enumerate((own, twin, other)):
         for b in range(batches):
             pool[1 + n * batches + b] = part[b]
     acc[...] = jnp.zeros_like(acc)
+    fetch.wait()
+    spread_ops(native, ops, scr)
+    to_smem.wait()
     blank = jnp.zeros(ops.shape[1:], BF16)
     low = lax.broadcasted_iota(I32, blank.shape, 1) < blank.shape[0]
 
     def group(g, _):
         blocks = []
         for h in range(GROUP):
-            op = ops[jnp.minimum(g * GROUP + h, last)]
+            op = ops[g * GROUP + h]
             blocks.append(jnp.concatenate([jnp.where(low, op, blank), jnp.where(low, blank, op)], axis=0))
         w = jnp.concatenate(blocks, axis=1)
         rows = []
@@ -139,10 +155,19 @@
         return 0
 
     lax.fori_loop(0, tbl.shape[1] // GROUP, group, 0)
-
-
-def far_kernel(slots, offs, items, arrived, ops, near, occ, out, pool, acc):
+    done = pltpu.make_async_copy(acc, sums, sems.at[0])
+    done.start()
+    done.wait()
+
+
+def far_kernel(slots, offs, items, arrived_hbm, ops, near_hbm, occ, out, arrived, near, pool, acc, sems):
     batches, pairs = near.shape[0], near.shape[1]
+    fetch = pltpu.make_async_copy(arrived_hbm, arrived, sems.at[0])
+    fetch_near = pltpu.make_async_copy(near_hbm, near, sems.at[1])
+    fetch.start()
+    fetch_near.start()
+    acc[...] = jnp.zeros_like(acc)
+    fetch.wait()
     half = ops.shape[1]
     pool[0] = jnp.zeros(pool.shape[1:], BF16)
 
@@ -153,8 +178,6 @@
         return 0
 
     lax.fori_loop(0, arrived.shape[0], fill, 0, unroll=8)
-    acc[0 : batches * pairs, :] = near[...].reshape(batches * pairs, LANES)
-    acc[batches * pairs :, :] = jnp.zeros((pairs, LANES), F32)
     low = lax.broadcasted_iota(I32, (pairs, LANES), 1) < half
     low_op = lax.broadcasted_iota(I32, (half, LANES), 1) < half
     total = lax.fori_loop(0, batches, lambda t, n: n + items[t, 0], 0)
@@ -179,6 +202,14 @@
         return t, g
 
     lax.fori_loop(0, (total + (ITEMS - 1)) // ITEMS, step, (jnp.int32(0), jnp.int32(0)))
+    fetch_near.wait()
+
+    def join(t, _):
+        at = pl.ds(pl.multiple_of(t * pairs, pairs), pairs)
+        acc[at, :] += near[t]
+        return 0
+
+    lax.fori_loop(0, batches, join, 0, unroll=8)
     cells = occ.shape[1]
     filled = occ[...].astype(F32).astype(BF16)
     cell = lax.broadcasted_iota(I32, (cells, LANES), 0)
@@ -201,14 +232,13 @@
     wide = padded(wide, 64)
     block = (pairs, LANES)
 
-    any_space = pl.BlockSpec(memory_space=pl.ANY)
     own, outgoing = pl.pallas_call(
         pack_kernel,
         out_shape=(
             jax.ShapeDtypeStruct((batches,) + block, BF16),
             jax.ShapeDtypeStruct((devices * slots,) + block, BF16),
         ),
-        in_specs=[SMEM, any_space, any_space],
+        in_specs=[SMEM, HBM, HBM],
         out_specs=(VMEM, VMEM),
         scratch_shapes=[
             pltpu.VMEM((batches, width), BF16),
@@ -227,52 +257,46 @@
     first = jnp.stack([me, me ^ 1, me - 1 + 2 * (me & 1)]) * batches
 
     tall = padded(batches + 1, 8)
-    near_tbl, far_slot, far_off, far_items = pl.pallas_call(
-        functools.partial(table_kernel, batches * devices),
+    sums, ops, far_slot, far_off, far_items = pl.pallas_call(
+        functools.partial(near_kernel, batches * devices),
         out_shape=(
-            jax.ShapeDtypeStruct((batches, wide), I32),
+            jax.ShapeDtypeStruct((batches,) + block, F32),
+            jax.ShapeDtypeStruct((wide, coeffs, LANES), BF16),
             jax.ShapeDtypeStruct((tall, wide), I32),
             jax.ShapeDtypeStruct((tall, wide), I32),
             jax.ShapeDtypeStruct((tall, LANES), I32),
         ),
-        in_specs=[SMEM, VMEM, VMEM, VMEM],
-        out_specs=(VMEM,) * 4,
-        compiler_params=params(16),
-        name="tables",
-    )(first, pair_source, pair_offset, live_pairs.reshape(1, batches))
-
-    ops = pl.pallas_call(
-        ops_kernel,
-        out_shape=jax.ShapeDtypeStruct((offsets, coeffs, LANES), BF16),
-        in_specs=[VMEM],
-        out_specs=VMEM,
-        scratch_shapes=[pltpu.VMEM((offsets * coeffs // 2, LANES), F32)],
-        compiler_params=params(24),
-        name="ops",
-    )(operators.transpose(1, 2, 0))
-    near = pl.pallas_call(
-        near_kernel,
-        out_shape=jax.ShapeDtypeStruct((batches,) + block, F32),
-        in_specs=[SMEM] + [VMEM] * 4,
-        out_specs=VMEM,
-        scratch_shapes=[pltpu.VMEM((3 * batches + 1,) + block, BF16)],
-        compiler_params=params(24),
+        in_specs=[SMEM, VMEM, VMEM, VMEM, HBM, VMEM, VMEM, VMEM],
+        out_specs=(HBM,) + (VMEM,) * 4,
+        scratch_shapes=[
+            pltpu.VMEM((coeffs, coeffs, offsets), BF16),
+            pltpu.VMEM((wide * coeffs // 2, LANES), F32),
+            pltpu.VMEM((batches, wide), I32),
+            pltpu.SMEM((batches, wide), I32),
+            pltpu.VMEM((3 * batches + 1,) + block, BF16),
+            pltpu.VMEM((batches,) + block, F32),
+            pltpu.SemaphoreType.DMA((2,)),
+        ],
+        compiler_params=params(28),
         cost_estimate=pl.CostEstimate(flops=12_000_000_000, bytes_accessed=4_000_000, transcendentals=0),
         name="near",
-    )(near_tbl, own, twin, other, ops)
+    )(first, pair_source, pair_offset, live_pairs.reshape(1, batches), operators.transpose(1, 2, 0), own, twin, other)
 
     return pl.pallas_call(
         far_kernel,
         out_shape=jax.ShapeDtypeStruct((batches, width), F32),
-        in_specs=[SMEM] * 3 + [VMEM] * 4,
+        in_specs=[SMEM] * 3 + [HBM, VMEM, HBM, VMEM],
         out_specs=VMEM,
         scratch_shapes=[
+            pltpu.VMEM((devices * slots,) + block, BF16),
+            pltpu.VMEM((batches,) + block, F32),
             pltpu.VMEM((devices * slots + 1, 2 * pairs, LANES), BF16),
             pltpu.VMEM(((batches + 1) * pairs, LANES), F32),
+            pltpu.SemaphoreType.DMA((2,)),
         ],
         compiler_params=params(32),
         name="far",
-    )(far_slot, far_off, far_items, arrived, ops, near, occupied)
+    )(far_slot, far_off, far_items, arrived, ops, sums, occupied)
 
 
 def solution(mesh):

time: 50.9 us -> 55.2 us (1.084)
  the two profiles are of different devices: /device:TPU:1 before, /device:TPU:14 now
where the time goes in v1:
time: 55.2 us; the launch traced here: 54.5 us
  Pallas kernels  33.3 us (60%)
  local copies, waits for them, and re-layouts  10.6 us (19%)
  starting transfers between devices  8.67 us (16%)
  waiting for transfers between devices  1.79 us (3%)
    pallas_call x1, Pallas kernels, local(): pl.pallas_call(functools.partial(near_kernel, batches * devices), out_sha...  22.5 us
    unnamed x26, local copies, waits for them, and re-layouts  10.6 us
    pallas_call x1, Pallas kernels, local(): pl.pallas_call(far_kernel, out_shape=jax.ShapeDtypeStruct((batches, width...  9.32 us
    all_to_all x1, starting transfers between devices, local(): lax.all_to_all(outgoing, axes, split_axis=0, concat_axis=0, tiled=True)  5.09 us
    ppermute x1, starting transfers between devices, local(): other = lax.ppermute(own, axes, odd)  1.92 us
    ppermute x1, waiting for transfers between devices, local(): other = lax.ppermute(own, axes, odd)  1.78 us
    ppermute x1, starting transfers between devices, local(): twin = lax.ppermute(own, axes, even)  1.66 us
    pallas_call x1, Pallas kernels, local(): pl.pallas_call(pack_kernel, out_shape=(jax.ShapeDtypeStruct((batches,) +...  1.51 us
  transfers between devices with their start and end apart: 3, of which 1 were waited for; matrix products, arithmetic and copies ran while one was open for 0% of the time, Pallas kernels for 41%

profile of v1, /device:TPU:14, one launch (start us, length us, event | category | flops | bytes accessed | tf_op | source)
XLA Modules:
  0.0 54.5 jit_solution(15835243442548277136)
XLA Ops:
  0.0 0.0 copy-start.2
  0.0 0.9 %copy-done.2 = bf16[32,4096]{1,0:T(8,128)(2,1)S(1)} copy-done((bf16[32,4096]{1,0:T(8,128)(2,1)S(1)}, bf16[32,4096]{1,0:T(8,128)(2,1)}, u32[]{:S(2)}) %copy-start.2) | copy-done | bytes 262168
  1.0 0.0 copy-start.3
  1.0 0.8 %copy-done.3 = s32[32,32,2]{1,2,0:T(2,128)S(1)} copy-done((s32[32,32,2]{1,2,0:T(2,128)S(1)}, s32[32,32,2]{1,2,0:T(2,128)}, u32[]{:S(2)}) %copy-start.3) | copy-done | bytes 8216
  1.7 1.5 %pack.1 = (bf16[32,32,128]{2,1,0:T(8,128)(2,1)S(1)}, bf16[64,32,128]{2,1,0:T(8,128)(2,1)}) custom-call(s32[1]{0:T(128)} %bitcast.me, s32[32,2,32]{2,1,0:T(2,128)S(1)} %bitcast.6, bf16[32,4096]{1,0:T(8,128)(2,1)S(1)} %copy-done.2), custom_call_target="tpu_custom_call" | custom-call | tf_op jit(solution)/shard_map/pack/pallas_call | solution.py:235
  3.2 1.9 %collective-permute-start.1 = (bf16[32,32,128]{2,1,0:T(8,128)(2,1)S(1)}, bf16[32,32,128]{2,1,0:T(8,128)(2,1)S(1)}, u32[]{:S(2)}, u32[]{:S(2)}) collective-permute-start(bf16[32,32,128]{2,1,0:T(8,128)(2,1)S(1)} %get-tuple-element.12.own), channel_id=1, source_target_pairs={{1,2},{2,1},{3,4},{4,3},{5,6},{6,5},{7,8},{8,7},{9,10},{10,9},{11,... | collective-permute-start | bytes 786440 | tf_op jit(solution)/shard_map/ppermute | solution.py:256
  5.2 1.7 %collective-permute-start = (bf16[32,32,128]{2,1,0:T(8,128)(2,1)S(1)}, bf16[32,32,128]{2,1,0:T(8,128)(2,1)S(1)}, u32[]{:S(2)}, u32[]{:S(2)}) collective-permute-start(bf16[32,32,128]{2,1,0:T(8,128)(2,1)S(1)} %get-tuple-element.12.own), channel_id=1, source_target_pairs={{0,1},{1,0},{2,3},{3,2},{4,5},{5,4},{6,7},{7,6},{8,9},{9,8},{10,11... | collective-permute-start | bytes 786440 | tf_op jit(solution)/shard_map/ppermute | solution.py:255
  6.8 5.1 %all-to-all-start = ((bf16[64,32,128]{2,1,0:T(8,128)(2,1)}), bf16[64,32,128]{2,1,0:T(8,128)(2,1)}, u32[]{:S(2)}, u32[]{:S(2)}) async-start(bf16[64,32,128]{2,1,0:T(8,128)(2,1)} %get-tuple-element.16), calls=%async_computation | async-start | bytes 1048576 | tf_op jit(solution)/shard_map/all_to_all | solution.py:254
  11.9 0.1 add_multiply_fusion.base
  12.0 1.8 %collective-permute-done.1.other = bf16[32,32,128]{2,1,0:T(8,128)(2,1)S(1)} collective-permute-done((bf16[32,32,128]{2,1,0:T(8,128)(2,1)S(1)}, bf16[32,32,128]{2,1,0:T(8,128)(2,1)S(1)}, u32[]{:S(2)}, u32[]{:S(2)}) %collective-permute-start.1) | collective-permute-done | bytes 262176 | tf_op jit(solution)/shard_map/ppermute | solution.py:256
  13.8 0.0 copy-start.6
  13.8 0.7 %copy-done.6 = bf16[32,32,128]{2,1,0:T(8,128)(2,1)} copy-done((bf16[32,32,128]{2,1,0:T(8,128)(2,1)}, bf16[32,32,128]{2,1,0:T(8,128)(2,1)S(1)}, u32[]{:S(2)}) %copy-start.6) | copy-done | bytes 262168
  14.5 0.0 collective-permute-done.twin
  14.5 0.0 copy-start.8
  14.5 0.7 %copy-done.8 = bf16[32,32,128]{2,1,0:T(8,128)(2,1)} copy-done((bf16[32,32,128]{2,1,0:T(8,128)(2,1)}, bf16[32,32,128]{2,1,0:T(8,128)(2,1)S(1)}, u32[]{:S(2)}) %copy-start.8) | copy-done | bytes 262168
  15.2 0.0 copy-start.5
  15.2 1.6 %copy-done.5 = bf16[189,64,64]{0,2,1:T(8,128)(2,1)S(1)} copy-done((bf16[189,64,64]{0,2,1:T(8,128)(2,1)S(1)}, bf16[189,64,64]{0,2,1:T(8,128)(2,1)}, u32[]{:S(2)}) %copy-start.5) | copy-done | bytes 1548312
  16.8 0.0 copy-start.7
  16.8 0.9 %copy-done.7 = bf16[32,32,128]{2,1,0:T(8,128)(2,1)S(1)} copy-done((bf16[32,32,128]{2,1,0:T(8,128)(2,1)S(1)}, bf16[32,32,128]{2,1,0:T(8,128)(2,1)}, u32[]{:S(2)}) %copy-start.7) | copy-done | bytes 262168
  17.7 0.0 copy-start.9
  17.7 0.9 %copy-done.9 = bf16[32,32,128]{2,1,0:T(8,128)(2,1)S(1)} copy-done((bf16[32,32,128]{2,1,0:T(8,128)(2,1)S(1)}, bf16[32,32,128]{2,1,0:T(8,128)(2,1)}, u32[]{:S(2)}) %copy-start.9) | copy-done | bytes 262168
  18.7 0.0 copy-start.10
  18.7 0.8 %copy-done.10 = s32[32,189]{1,0:T(8,128)S(1)} copy-done((s32[32,189]{1,0:T(8,128)S(1)}, s32[32,189]{1,0:T(8,128)}, u32[]{:S(2)}) %copy-start.10) | copy-done | bytes 24216
  19.4 0.0 copy-start.11
  19.4 0.8 %copy-done.11 = s32[32,189]{1,0:T(8,128)S(1)} copy-done((s32[32,189]{1,0:T(8,128)S(1)}, s32[32,189]{1,0:T(8,128)}, u32[]{:S(2)}) %copy-start.11) | copy-done | bytes 24216
  20.2 0.0 copy-start.12
  20.2 0.7 %copy-done.12 = s32[32]{0:T(128)S(1)} copy-done((s32[32]{0:T(128)S(1)}, s32[32]{0:T(128)}, u32[]{:S(2)}) %copy-start.12) | copy-done | bytes 152
  20.9 0.0 copy-start.4
  20.9 22.5 %near.1 = (f32[32,32,128]{2,1,0:T(8,128)S(1)}, bf16[192,64,128]{2,1,0:T(8,128)(2,1)S(1)}, s32[40,192]{1,0:T(8,128)S(1)}, s32[40,192]{1,0:T(8,128)S(1)}, s32[40,128]{1,0:T(8,128)S(1)}) custom-call(s32[3]{0:T(128)S(1)} %add_multiply_fusion.base, s32[32,189]{1,0:T(8,128)S(1)} %copy-done.10, s32[32,189]{1,0:T(8,128)S(1)} %copy-done.11, s32[1,32]{1,0:T(1,128)S(1)} %bitcast.8, ...), custom_call_target="tpu_custom_call" | custom-call | flops 12000000000 | bytes 4000000 | tf_op jit(solution)/shard_map/near/pallas_call | solution.py:260
  43.4 0.0 copy-start
  43.4 0.8 %copy-done = f32[32,32,128]{2,1,0:T(8,128)} copy-done((f32[32,32,128]{2,1,0:T(8,128)}, f32[32,32,128]{2,1,0:T(8,128)S(1)}, u32[]{:S(2)}) %copy-start) | copy-done | bytes 524312
  44.2 0.0 all-to-all-done.arrived_hbm
  44.2 0.0 copy-done.4
  44.2 0.0 copy-start.1
  44.2 1.0 %copy-done.1 = f32[32,32,128]{2,1,0:T(8,128)S(1)} copy-done((f32[32,32,128]{2,1,0:T(8,128)S(1)}, f32[32,32,128]{2,1,0:T(8,128)}, u32[]{:S(2)}) %copy-start.1) | copy-done | bytes 524312
  45.2 9.3 %far.1 = f32[32,4096]{1,0:T(8,128)} custom-call(s32[40,192]{1,0:T(8,128)S(1)} %get-tuple-element.13.slots, s32[40,192]{1,0:T(8,128)S(1)} %get-tuple-element.14.offs, s32[40,128]{1,0:T(8,128)S(1)} %get-tuple-element.15.items, bf16[64,32,128]{2,1,0:T(8,128)(2,1)} %all-to-all-done.arrived_hbm, bf16[192,64,128]{2,1,0:T(8,128)(2,1)S(1)} %get-tuple-element.17.ops, ...), custom_call_target="tpu_custom_call" | custom-call | tf_op jit(solution)/shard_map/far/pallas_call | solution.py:285
Async XLA Ops:
  0.0 0.9 %copy-start.2 = (bf16[32,4096]{1,0:T(8,128)(2,1)S(1)}, bf16[32,4096]{1,0:T(8,128)(2,1)}, u32[]{:S(2)}) copy-start(bf16[32,4096]{1,0:T(8,128)(2,1)} %m_hbm.1) | copy-start | bytes 786436
  1.0 0.8 %copy-start.3 = (s32[32,32,2]{1,2,0:T(2,128)S(1)}, s32[32,32,2]{1,2,0:T(2,128)}, u32[]{:S(2)}) copy-start(s32[32,32,2]{1,2,0:T(2,128)} %param.12) | copy-start | bytes 24580
  3.2 10.5 %collective-permute-start.1 = (bf16[32,32,128]{2,1,0:T(8,128)(2,1)S(1)}, bf16[32,32,128]{2,1,0:T(8,128)(2,1)S(1)}, u32[]{:S(2)}, u32[]{:S(2)}) collective-permute-start(bf16[32,32,128]{2,1,0:T(8,128)(2,1)S(1)} %get-tuple-element.12.own), channel_id=1, source_target_pairs={{1,2},{2,1},{3,4},{4,3},{5,6},{6,5},{7,8},{8,7},{9,10},{10,9},{11,... | collective-permute-start | bytes 786440 | tf_op jit(solution)/shard_map/ppermute | solution.py:256
  5.2 9.3 %collective-permute-start = (bf16[32,32,128]{2,1,0:T(8,128)(2,1)S(1)}, bf16[32,32,128]{2,1,0:T(8,128)(2,1)S(1)}, u32[]{:S(2)}, u32[]{:S(2)}) collective-permute-start(bf16[32,32,128]{2,1,0:T(8,128)(2,1)S(1)} %get-tuple-element.12.own), channel_id=1, source_target_pairs={{0,1},{1,0},{2,3},{3,2},{4,5},{5,4},{6,7},{7,6},{8,9},{9,8},{10,11... | collective-permute-start | bytes 786440 | tf_op jit(solution)/shard_map/ppermute | solution.py:255
  6.8 37.3 %all-to-all-start = ((bf16[64,32,128]{2,1,0:T(8,128)(2,1)}), bf16[64,32,128]{2,1,0:T(8,128)(2,1)}, u32[]{:S(2)}, u32[]{:S(2)}) async-start(bf16[64,32,128]{2,1,0:T(8,128)(2,1)} %get-tuple-element.16), calls=%async_computation | async-start | bytes 1048576 | tf_op jit(solution)/shard_map/all_to_all | solution.py:254
  13.8 0.7 %copy-start.6 = (bf16[32,32,128]{2,1,0:T(8,128)(2,1)}, bf16[32,32,128]{2,1,0:T(8,128)(2,1)S(1)}, u32[]{:S(2)}) copy-start(bf16[32,32,128]{2,1,0:T(8,128)(2,1)S(1)} %collective-permute-done.1.other) | copy-start | bytes 786436
  14.5 0.7 %copy-start.8 = (bf16[32,32,128]{2,1,0:T(8,128)(2,1)}, bf16[32,32,128]{2,1,0:T(8,128)(2,1)S(1)}, u32[]{:S(2)}) copy-start(bf16[32,32,128]{2,1,0:T(8,128)(2,1)S(1)} %collective-permute-done.twin) | copy-start | bytes 786436
  15.2 1.6 %copy-start.5 = (bf16[189,64,64]{0,2,1:T(8,128)(2,1)S(1)}, bf16[189,64,64]{0,2,1:T(8,128)(2,1)}, u32[]{:S(2)}) copy-start(bf16[189,64,64]{0,2,1:T(8,128)(2,1)} %param.8) | copy-start | bytes 4644868
  16.8 0.9 %copy-start.7 = (bf16[32,32,128]{2,1,0:T(8,128)(2,1)S(1)}, bf16[32,32,128]{2,1,0:T(8,128)(2,1)}, u32[]{:S(2)}) copy-start(bf16[32,32,128]{2,1,0:T(8,128)(2,1)} %copy-done.6) | copy-start | bytes 786436
  17.7 0.9 %copy-start.9 = (bf16[32,32,128]{2,1,0:T(8,128)(2,1)S(1)}, bf16[32,32,128]{2,1,0:T(8,128)(2,1)}, u32[]{:S(2)}) copy-start(bf16[32,32,128]{2,1,0:T(8,128)(2,1)} %copy-done.8) | copy-start | bytes 786436
  18.7 0.8 %copy-start.10 = (s32[32,189]{1,0:T(8,128)S(1)}, s32[32,189]{1,0:T(8,128)}, u32[]{:S(2)}) copy-start(s32[32,189]{1,0:T(8,128)} %src.1) | copy-start | bytes 72580
  19.4 0.8 %copy-start.11 = (s32[32,189]{1,0:T(8,128)S(1)}, s32[32,189]{1,0:T(8,128)}, u32[]{:S(2)}) copy-start(s32[32,189]{1,0:T(8,128)} %off.1) | copy-start | bytes 72580
  20.2 0.7 %copy-start.12 = (s32[32]{0:T(128)S(1)}, s32[32]{0:T(128)}, u32[]{:S(2)}) copy-start(s32[32]{0:T(128)} %param.11) | copy-start | bytes 388
  20.9 23.3 %copy-start.4 = (s32[32,64]{1,0:T(8,128)S(1)}, s32[32,64]{1,0:T(8,128)}, u32[]{:S(2)}) copy-start(s32[32,64]{1,0:T(8,128)} %occ.1) | copy-start | bytes 24580
  43.4 0.8 %copy-start = (f32[32,32,128]{2,1,0:T(8,128)}, f32[32,32,128]{2,1,0:T(8,128)S(1)}, u32[]{:S(2)}) copy-start(f32[32,32,128]{2,1,0:T(8,128)S(1)} %get-tuple-element.18.near_hbm) | copy-start | bytes 1572868
  44.2 1.0 %copy-start.1 = (f32[32,32,128]{2,1,0:T(8,128)S(1)}, f32[32,32,128]{2,1,0:T(8,128)}, u32[]{:S(2)}) copy-start(f32[32,32,128]{2,1,0:T(8,128)} %copy-done) | copy-start | bytes 1572868

commit v2 on v1

--- a/solution.py
+++ b/solution.py
@@ -14,6 +14,7 @@
 SMEM = pl.BlockSpec(memory_space=pltpu.SMEM)
 HBM = pl.BlockSpec(memory_space=pltpu.HBM)
 GROUP = 16
+SLOTS = 16
 FEW = 8
 ITEMS = 16
 LANES = 128
@@ -59,15 +60,17 @@
     tall = twice.shape[0]
     at = lax.broadcasted_iota(I32, (tall, offsets), 0)
     eye = jnp.where(at == lax.broadcasted_iota(I32, (tall, offsets), 1), 1.0, 0.0).astype(BF16)
-    for i in range(0, half, 2):
-        x = jnp.concatenate([native[i], native[half + i], native[i + 1], native[half + i + 1]], axis=0)
-        y = lax.dot_general(eye, x, NT, preferred_element_type=F32)
-        scr[pl.ds(i, tall, stride=half), :] = y[:, :LANES]
-        scr[pl.ds(i + 1, tall, stride=half), :] = y[:, LANES:]
+    for i in range(0, half, 8):
+        found = []
+        for k in range(i, i + 8, 2):
+            x = jnp.concatenate([native[k], native[half + k], native[k + 1], native[half + k + 1]], axis=0)
+            y = lax.dot_general(eye, x, NT, preferred_element_type=F32)
+            found += [y[:, :LANES], y[:, LANES:]]
+        scr[:, i : i + 8, :] = jnp.swapaxes(jnp.stack(found, axis=0), 0, 1)
     low = lax.broadcasted_iota(I32, (half, LANES), 1) < coeffs
 
     def spread(l, _):
-        x = scr[pl.ds(pl.multiple_of(l * half, half), half), :]
+        x = scr[l]
         y = pltpu.roll(x, coeffs, 1)
         twice[l, 0:half] = jnp.where(low, x, y).astype(BF16)
         twice[l, half:coeffs] = jnp.where(low, y, x).astype(BF16)
@@ -76,9 +79,13 @@
     lax.fori_loop(0, tall, spread, 0, unroll=8)
 
 
-def make_tables(total_batches, base, src, off, live, near_tbl, far_slot, far_off, far_items):
+def one_hot(want, row):
+    return jnp.where(want == row, 1.0, 0.0).astype(BF16)
+
+
+def make_tables(total_batches, base, src, off, live, near_slots, late_slot, late_off, late_items):
     rows, lst = src.shape
-    wide = near_tbl.shape[1]
+    slots, wide = SLOTS, near_slots.shape[0]
     s = src[...]
     o = off[...]
     mine = base[0]
@@ -87,97 +94,143 @@
     at_r = lax.broadcasted_iota(I32, (rows, rows), 0)
     at_c = lax.broadcasted_iota(I32, (rows, rows), 1)
     count_col = jnp.sum(jnp.where(at_r == at_c, live[...], 0), axis=1, keepdims=True)
-    col = lax.broadcasted_iota(I32, (rows, lst), 1)
-    alive = col < count_col
+    alive = lax.broadcasted_iota(I32, (rows, lst), 1) < count_col
     far = s >= total_batches
     in_mine = (s >= mine) & (s < mine + rows)
     in_twin = (s >= twin) & (s < twin + rows)
     place = jnp.where(in_mine, s - mine, jnp.where(in_twin, s - twin + rows, s - other + 2 * rows))
-    near_val = jnp.where(alive & jnp.logical_not(far), place + 1, 0)
-    far_live = alive & far
-    far_val = jnp.where(far_live, s - total_batches + 1, 0)
-    one = jnp.where(far_live, 1.0, 0.0)
-    before = lax.broadcasted_iota(I32, (lst, lst), 0) < lax.broadcasted_iota(I32, (lst, lst), 1)
-    rank = jnp.dot(one.astype(BF16), jnp.where(before, 1.0, 0.0).astype(BF16), preferred_element_type=F32)
-    pos = jnp.where(far_live, rank.astype(I32), wide)
+    place = jnp.where(far, s - total_batches + 3 * rows, place)
+    value = jnp.where(alive, place + 1, 0)
+    both = jnp.concatenate([value & 127, value >> 7], axis=0).astype(F32).astype(BF16)
+    want = lax.broadcasted_iota(I32, (wide, lst), 0)
+    lows, highs = [], []
+    for t in range(rows):
+        got = lax.dot_general(both, one_hot(want, o[t : t + 1, :]), NT, preferred_element_type=F32)
+        lows.append(got[t : t + 1, :])
+        highs.append(got[rows + t : rows + t + 1, :])
+    low = jnp.concatenate(lows, axis=0)
+    high = jnp.concatenate(highs, axis=0)
+    value = (low + 128.0 * high).astype(I32)
+    near = (value > 0) & (value <= 3 * rows)
+    sooner = jnp.where(at_c < at_r, 1.0, 0.0).astype(BF16)
+    rank = jnp.dot(sooner, jnp.where(near, 1.0, 0.0).astype(BF16), preferred_element_type=F32).astype(I32)
+    target = lax.broadcasted_iota(I32, (rows, wide), 0)
+    sources, targets = [], []
+    for r in range(slots):
+        sel = near & (rank == r)
+        sources.append(jnp.sum(jnp.where(sel, value, 0), axis=0, keepdims=True))
+        targets.append(jnp.sum(jnp.where(sel, target - rows, 0), axis=0, keepdims=True) + rows)
+    table = jnp.concatenate(sources + targets, axis=0).astype(F32)
+    near_slots[:, 0 : 2 * slots] = table.T.astype(I32)
+    late = (value > 3 * rows) | (near & (rank >= slots))
+    one = jnp.where(late, 1.0, 0.0)
+    before = lax.broadcasted_iota(I32, (wide, wide), 0) < lax.broadcasted_iota(I32, (wide, wide), 1)
+    order = jnp.dot(one.astype(BF16), jnp.where(before, 1.0, 0.0).astype(BF16), preferred_element_type=F32)
+    pos = jnp.where(late, order.astype(I32), wide)
     count = jnp.sum(one, axis=1, keepdims=True).astype(I32)
     items = jnp.maximum((count + (FEW - 1)) // FEW, 1)
-    far_items[...] = jnp.ones_like(far_items)
-    far_items[0:rows, :] = jnp.broadcast_to(items, (rows, LANES))
-    near_b = near_val.astype(F32).astype(BF16)
-    far_b = jnp.concatenate([far_val & 127, far_val >> 7, o], axis=0).astype(F32).astype(BF16)
-    want = lax.broadcasted_iota(I32, (wide, lst), 0)
-    far_slot[...] = jnp.zeros_like(far_slot)
-    far_off[...] = jnp.zeros_like(far_off)
+    late_items[...] = jnp.ones_like(late_items)
+    late_items[0:rows, :] = jnp.broadcast_to(items, (rows, LANES))
+    late_slot[...] = jnp.zeros_like(late_slot)
+    late_off[...] = jnp.zeros_like(late_off)
+    want = lax.broadcasted_iota(I32, (wide, wide), 0)
+    offset = lax.broadcasted_iota(I32, (16, wide), 1).astype(F32)
+    parts = jnp.concatenate([low, high, offset], axis=0).astype(BF16)
     for t in range(rows):
-        hot = jnp.where(want == o[t : t + 1, :], 1.0, 0.0).astype(BF16)
-        got = lax.dot_general(near_b, hot, NT, preferred_element_type=F32)
-        near_tbl[t : t + 1, :] = got[t : t + 1, :].astype(I32)
-        hot = jnp.where(want == pos[t : t + 1, :], 1.0, 0.0).astype(BF16)
-        got = lax.dot_general(far_b, hot, NT, preferred_element_type=F32).astype(I32)
-        far_slot[t : t + 1, :] = got[t : t + 1, :] + 128 * got[rows + t : rows + t + 1, :]
-        far_off[t : t + 1, :] = got[2 * rows + t : 2 * rows + t + 1, :]
+        got = lax.dot_general(parts, one_hot(want, pos[t : t + 1, :]), NT, preferred_element_type=F32).astype(I32)
+        late_slot[t : t + 1, :] = got[t : t + 1, :] + 128 * got[rows + t : rows + t + 1, :]
+        late_off[t : t + 1, :] = got[2 * rows : 2 * rows + 1, :]
 
 
 def near_kernel(
     total_batches, base, src, off, live, native_hbm, own, twin, other,
-    sums, ops, far_slot, far_off, far_items,
-    native, scr, tbl_v, tbl, pool, acc, sems,
+    sums, ops_hbm, late_slot, late_off, late_items,
+    native, scr, ops, slots_v, slot_t, pool, acc_a, acc_b, acc_c, acc_d, sems,
 ):
     fetch = pltpu.make_async_copy(native_hbm, native, sems.at[0])
     fetch.start()
-    make_tables(total_batches, base, src, off, live, tbl_v, far_slot, far_off, far_items)
-    to_smem = pltpu.make_async_copy(tbl_v, tbl, sems.at[1])
+    make_tables(total_batches, base, src, off, live, slots_v, late_slot, late_off, late_items)
+    to_smem = pltpu.make_async_copy(slots_v, slot_t, sems.at[1])
     to_smem.start()
-    batches = own.shape[0]
+    batches, pairs = own.shape[0], own.shape[1]
     pool[0] = jnp.zeros(pool.shape[1:], BF16)
     for n, part in enumerate((own, twin, other)):
         for b in range(batches):
             pool[1 + n * batches + b] = part[b]
-    acc[...] = jnp.zeros_like(acc)
+    accs = (acc_a, acc_b, acc_c, acc_d)
+    for acc in accs:
+        acc[...] = jnp.zeros_like(acc)
     fetch.wait()
     spread_ops(native, ops, scr)
+    keep = pltpu.make_async_copy(ops, ops_hbm, sems.at[2])
+    keep.start()
     to_smem.wait()
+    slots = SLOTS
     blank = jnp.zeros(ops.shape[1:], BF16)
+    none = jnp.zeros((2 * blank.shape[0], LANES), BF16)
     low = lax.broadcasted_iota(I32, blank.shape, 1) < blank.shape[0]
 
+    def twice(l):
+        op = ops[l]
+        return jnp.concatenate([jnp.where(low, op, blank), jnp.where(low, blank, op)], axis=0)
+
     def group(g, _):
-        blocks = []
-        for h in range(GROUP):
-            op = ops[g * GROUP + h]
-            blocks.append(jnp.concatenate([jnp.where(low, op, blank), jnp.where(low, blank, op)], axis=0))
-        w = jnp.concatenate(blocks, axis=1)
-        rows = []
-        for t in range(batches):
-            rows.append(jnp.concatenate([pool[tbl[t, g * GROUP + h]] for h in range(GROUP)], axis=1))
-        x = jnp.concatenate(rows, axis=0)
-        acc[...] += lax.dot_general(x, w, NT, preferred_element_type=F32).reshape(acc.shape)
-        return 0
-
-    lax.fori_loop(0, tbl.shape[1] // GROUP, group, 0)
-    done = pltpu.make_async_copy(acc, sums, sems.at[0])
+        for h in range(0, GROUP, 2):
+            l = g * GROUP + h
+            top = jnp.concatenate([twice(l), none], axis=1)
+            end = jnp.concatenate([none, twice(l + 1)], axis=1)
+            w = jnp.concatenate([top, end], axis=0)
+            rows = [jnp.concatenate([pool[slot_t[l, r]], pool[slot_t[l + 1, r]]], axis=1) for r in range(slots)]
+            y = lax.dot_general(jnp.concatenate(rows, axis=0), w, NT, preferred_element_type=F32)
+            for side in range(2):
+                acc = accs[(h % 4) // 2 * 2 + side]
+                for r in range(0, slots, 4):
+                    ats = [slot_t[l + side, slots + r + k] for k in range(4)]
+                    olds = [acc[at] for at in ats]
+                    for k in range(4):
+                        new = y[(r + k) * pairs : (r + k + 1) * pairs, side * LANES : (side + 1) * LANES]
+                        acc[ats[k]] = olds[k] + new
+        return 0
+
+    lax.fori_loop(0, slot_t.shape[0] // GROUP, group, 0)
+
+    def join(t, _):
+        acc_a[t] = (acc_a[t] + acc_b[t]) + (acc_c[t] + acc_d[t])
+        return 0
+
+    lax.fori_loop(0, batches, join, 0, unroll=8)
+    done = pltpu.make_async_copy(acc_a.at[0:batches], sums, sems.at[0])
     done.start()
+    keep.wait()
     done.wait()
 
 
-def far_kernel(slots, offs, items, arrived_hbm, ops, near_hbm, occ, out, arrived, near, pool, acc, sems):
+def far_kernel(slots, offs, items, own, twin, other, arrived_hbm, ops_hbm, near_hbm, occ, out, arrived, ops, near, pool, acc, sems):
     batches, pairs = near.shape[0], near.shape[1]
     fetch = pltpu.make_async_copy(arrived_hbm, arrived, sems.at[0])
     fetch_near = pltpu.make_async_copy(near_hbm, near, sems.at[1])
+    fetch_ops = pltpu.make_async_copy(ops_hbm, ops, sems.at[2])
     fetch.start()
+    fetch_ops.start()
     fetch_near.start()
     acc[...] = jnp.zeros_like(acc)
-    fetch.wait()
     half = ops.shape[1]
     pool[0] = jnp.zeros(pool.shape[1:], BF16)
 
-    def fill(n, _):
-        x = arrived[n]
-        pool[n + 1, 0:pairs] = x
-        pool[n + 1, pairs : 2 * pairs] = jnp.concatenate([x[:, half:], x[:, :half]], axis=1)
-        return 0
-
-    lax.fori_loop(0, arrived.shape[0], fill, 0, unroll=8)
+    def fill(part, start):
+        def put(n, _):
+            x = part[n]
+            pool[start + n, 0:pairs] = x
+            pool[start + n, pairs : 2 * pairs] = jnp.concatenate([x[:, half:], x[:, :half]], axis=1)
+            return 0
+
+        lax.fori_loop(0, part.shape[0], put, 0, unroll=8)
+
+    for n, part in enumerate((own, twin, other)):
+        fill(part, 1 + n * batches)
+    fetch.wait()
+    fill(arrived, 1 + 3 * batches)
+    fetch_ops.wait()
     low = lax.broadcasted_iota(I32, (pairs, LANES), 1) < half
     low_op = lax.broadcasted_iota(I32, (half, LANES), 1) < half
     total = lax.fori_loop(0, batches, lambda t, n: n + items[t, 0], 0)
@@ -246,7 +299,7 @@
             pltpu.VMEM((batches * pairs, LANES), F32),
             pltpu.SemaphoreType.DMA((2,)),
         ],
-        compiler_params=params(16),
+        compiler_params=params(56),
         name="pack",
     )(me.reshape(1), send_lists.transpose(0, 2, 1), multipoles)
     even = [(i, i ^ 1) for i in range(devices)]
@@ -257,7 +310,7 @@
     first = jnp.stack([me, me ^ 1, me - 1 + 2 * (me & 1)]) * batches
 
     tall = padded(batches + 1, 8)
-    sums, ops, far_slot, far_off, far_items = pl.pallas_call(
+    sums, ops, late_slot, late_off, late_items = pl.pallas_call(
         functools.partial(near_kernel, batches * devices),
         out_shape=(
             jax.ShapeDtypeStruct((batches,) + block, F32),
@@ -267,17 +320,20 @@
             jax.ShapeDtypeStruct((tall, LANES), I32),
         ),
         in_specs=[SMEM, VMEM, VMEM, VMEM, HBM, VMEM, VMEM, VMEM],
-        out_specs=(HBM,) + (VMEM,) * 4,
+        out_specs=(HBM, HBM) + (VMEM,) * 3,
         scratch_shapes=[
             pltpu.VMEM((coeffs, coeffs, offsets), BF16),
-            pltpu.VMEM((wide * coeffs // 2, LANES), F32),
-            pltpu.VMEM((batches, wide), I32),
-            pltpu.SMEM((batches, wide), I32),
+            pltpu.VMEM((wide, coeffs // 2, LANES), F32),
+            pltpu.VMEM((wide, coeffs, LANES), BF16),
+            pltpu.VMEM((wide, LANES), I32),
+            pltpu.SMEM((wide, LANES), I32),
             pltpu.VMEM((3 * batches + 1,) + block, BF16),
-            pltpu.VMEM((batches,) + block, F32),
-            pltpu.SemaphoreType.DMA((2,)),
+        ]
+        + [pltpu.VMEM((batches + 1,) + block, F32)] * 4
+        + [
+            pltpu.SemaphoreType.DMA((3,)),
         ],
-        compiler_params=params(28),
+        compiler_params=params(56),
         cost_estimate=pl.CostEstimate(flops=12_000_000_000, bytes_accessed=4_000_000, transcendentals=0),
         name="near",
     )(first, pair_source, pair_offset, live_pairs.reshape(1, batches), operators.transpose(1, 2, 0), own, twin, other)
@@ -285,18 +341,19 @@
     return pl.pallas_call(
         far_kernel,
         out_shape=jax.ShapeDtypeStruct((batches, width), F32),
-        in_specs=[SMEM] * 3 + [HBM, VMEM, HBM, VMEM],
+        in_specs=[SMEM] * 3 + [VMEM] * 3 + [HBM] * 3 + [VMEM],
         out_specs=VMEM,
         scratch_shapes=[
             pltpu.VMEM((devices * slots,) + block, BF16),
+            pltpu.VMEM((wide, coeffs, LANES), BF16),
             pltpu.VMEM((batches,) + block, F32),
-            pltpu.VMEM((devices * slots + 1, 2 * pairs, LANES), BF16),
+            pltpu.VMEM((3 * batches + devices * slots + 1, 2 * pairs, LANES), BF16),
             pltpu.VMEM(((batches + 1) * pairs, LANES), F32),
-            pltpu.SemaphoreType.DMA((2,)),
+            pltpu.SemaphoreType.DMA((3,)),
         ],
-        compiler_params=params(32),
+        compiler_params=params(56),
         name="far",
-    )(far_slot, far_off, far_items, arrived, ops, sums, occupied)
+    )(late_slot, late_off, late_items, own, twin, other, arrived, ops, sums, occupied)
 
 
 def solution(mesh):

time: 55.2 us -> 47.1 us (0.85)
  local copies, waits for them, and re-layouts: 10.6 us -> 1.59 us
  waiting for transfers between devices: 1.79 us -> 2.83 us
  Pallas kernels: 33.3 us -> 32.7 us
    unnamed x26 -> x6, local copies, waits for them, and re-layouts: 10.6 us -> 1.59 us
    pallas_call x1, Pallas kernels: 22.5 us -> 21.3 us  [local(): pl.pallas_call(functools.partial(near_kernel, batches * devices), out_sha...]
    ppermute x1, waiting for transfers between devices: 1.78 us -> 2.83 us  [local(): other = lax.ppermute(own, axes, odd)]
    pallas_call x1, Pallas kernels: 1.51 us -> 2.5 us  [local(): pl.pallas_call(pack_kernel, out_shape=(jax.ShapeDtypeStruct((batches,) +...]
  transfers between devices with their start and end apart: 3 -> 3, of which waited for: 1 -> 1; matrix products, arithmetic and copies ran while one was open for 0% -> 1% of each run, Pallas kernels for 41% -> 46%
where the time goes in v2:
time: 47.1 us; the launch traced here: 46.4 us
  Pallas kernels  32.7 us (69%)
  starting transfers between devices  8.61 us (18%)
  waiting for transfers between devices  2.83 us (6%)
  local copies, waits for them, and re-layouts  1.59 us (3%)
  other arithmetic  0.59 us (1%)
    pallas_call x1, Pallas kernels, local(): pl.pallas_call(functools.partial(near_kernel, batches * devices), out_sha...  21.3 us
    pallas_call x1, Pallas kernels, local(): pl.pallas_call(far_kernel, out_shape=jax.ShapeDtypeStruct((batches, width...  8.91 us
    all_to_all x1, starting transfers between devices, local(): lax.all_to_all(outgoing, axes, split_axis=0, concat_axis=0, tiled=True)  5.03 us
    ppermute x1, waiting for transfers between devices, local(): other = lax.ppermute(own, axes, odd)  2.83 us
    pallas_call x1, Pallas kernels, local(): pl.pallas_call(pack_kernel, out_shape=(jax.ShapeDtypeStruct((batches,) +...  2.5 us
    ppermute x1, starting transfers between devices, local(): other = lax.ppermute(own, axes, odd)  1.92 us
    ppermute x1, starting transfers between devices, local(): twin = lax.ppermute(own, axes, even)  1.66 us
    unnamed x6, local copies, waits for them, and re-layouts  1.59 us
  transfers between devices with their start and end apart: 3, of which 1 were waited for; matrix products, arithmetic and copies ran while one was open for 1% of the time, Pallas kernels for 46%

profile of v2, /device:TPU:14, one launch (start us, length us, event | category | flops | bytes accessed | tf_op | source)
XLA Modules:
  0.0 46.4 jit_solution(2218514430990018832)
XLA Ops:
  0.0 2.5 %pack.1 = (bf16[32,32,128]{2,1,0:T(8,128)(2,1)}, bf16[64,32,128]{2,1,0:T(8,128)(2,1)}) custom-call(s32[1]{0:T(128)} %bitcast.me, s32[32,2,32]{2,1,0:T(2,128)} %bitcast.6, bf16[32,4096]{1,0:T(8,128)(2,1)} %m_hbm.1), custom_call_target="tpu_custom_call" | custom-call | tf_op jit(solution)/shard_map/pack/pallas_call | solution.py:288
  2.5 1.9 %collective-permute-start.1 = (bf16[32,32,128]{2,1,0:T(8,128)(2,1)}, bf16[32,32,128]{2,1,0:T(8,128)(2,1)S(1)}, u32[]{:S(2)}, u32[]{:S(2)}) collective-permute-start(bf16[32,32,128]{2,1,0:T(8,128)(2,1)} %get-tuple-element.12.own), channel_id=1, source_target_pairs={{1,2},{2,1},{3,4},{4,3},{5,6},{6,5},{7,8},{8,7},{9,10},{10,9},{11,... | collective-permute-start | bytes 786440 | tf_op jit(solution)/shard_map/ppermute | solution.py:309
  4.4 1.7 %collective-permute-start = (bf16[32,32,128]{2,1,0:T(8,128)(2,1)}, bf16[32,32,128]{2,1,0:T(8,128)(2,1)S(1)}, u32[]{:S(2)}, u32[]{:S(2)}) collective-permute-start(bf16[32,32,128]{2,1,0:T(8,128)(2,1)} %get-tuple-element.12.own), channel_id=1, source_target_pairs={{0,1},{1,0},{2,3},{3,2},{4,5},{5,4},{6,7},{7,6},{8,9},{9,8},{10,11... | collective-permute-start | bytes 786440 | tf_op jit(solution)/shard_map/ppermute | solution.py:308
  6.1 5.0 %all-to-all-start = ((bf16[64,32,128]{2,1,0:T(8,128)(2,1)}), bf16[64,32,128]{2,1,0:T(8,128)(2,1)S(1)}, u32[]{:S(2)}, u32[]{:S(2)}) async-start(bf16[64,32,128]{2,1,0:T(8,128)(2,1)} %get-tuple-element.16), calls=%async_computation | async-start | bytes 1048576 | tf_op jit(solution)/shard_map/all_to_all | solution.py:307
  11.1 0.6 %add_multiply_fusion.base = s32[3]{0:T(128)} fusion(s32[1]{0:T(128)} %bitcast.2, s32[1]{0:T(128)} %bitcast.1, s32[1]{0:T(128)} %bitcast.me), kind=kLoop, calls=%fused_computation | loop fusion | flops 9 | bytes 24 | tf_op jit(solution)/shard_map/mul | solution.py:310
  11.7 2.8 %collective-permute-done.1.other = bf16[32,32,128]{2,1,0:T(8,128)(2,1)S(1)} collective-permute-done((bf16[32,32,128]{2,1,0:T(8,128)(2,1)}, bf16[32,32,128]{2,1,0:T(8,128)(2,1)S(1)}, u32[]{:S(2)}, u32[]{:S(2)}) %collective-permute-start.1) | collective-permute-done | bytes 262176 | tf_op jit(solution)/shard_map/ppermute | solution.py:309
  14.6 0.0 copy-start.1
  14.6 0.0 collective-permute-done.twin
  14.6 0.0 copy-start.2
  14.6 0.7 %copy-done.1 = bf16[32,32,128]{2,1,0:T(8,128)(2,1)} copy-done((bf16[32,32,128]{2,1,0:T(8,128)(2,1)}, bf16[32,32,128]{2,1,0:T(8,128)(2,1)S(1)}, u32[]{:S(2)}) %copy-start.1) | copy-done | bytes 262168
  15.3 0.1 copy-done.2
  15.4 21.3 %near.1 = (f32[32,32,128]{2,1,0:T(8,128)}, bf16[192,64,128]{2,1,0:T(8,128)(2,1)}, s32[40,192]{1,0:T(8,128)}, s32[40,192]{1,0:T(8,128)}, s32[40,128]{1,0:T(8,128)}) custom-call(s32[3]{0:T(128)} %add_multiply_fusion.base, s32[32,189]{1,0:T(8,128)} %src.1, s32[32,189]{1,0:T(8,128)} %off.1, s32[1,32]{1,0:T(1,128)} %bitcast.8, bf16[64,64,189]{2,1,0:T(8,128)(2,1)} %bitcast.7, ...), custom_call_target="tpu_custom_call" | custom-call | flops 12000000000 | bytes 4000000 | tf_op jit(solution)/shard_map/near/pallas_call | solution.py:313
  36.7 0.0 all-to-all-done.arrived_hbm
  36.7 0.0 copy-start
  36.7 0.8 %copy-done = bf16[64,32,128]{2,1,0:T(8,128)(2,1)} copy-done((bf16[64,32,128]{2,1,0:T(8,128)(2,1)}, bf16[64,32,128]{2,1,0:T(8,128)(2,1)S(1)}, u32[]{:S(2)}) %copy-start) | copy-done | bytes 524312
  37.5 8.9 %far.1 = f32[32,4096]{1,0:T(8,128)} custom-call(s32[40,192]{1,0:T(8,128)} %get-tuple-element.13.slots, s32[40,192]{1,0:T(8,128)} %get-tuple-element.14.offs, s32[40,128]{1,0:T(8,128)} %get-tuple-element.15.items, bf16[32,32,128]{2,1,0:T(8,128)(2,1)} %get-tuple-element.12.own, bf16[32,32,128]{2,1,0:T(8,128)(2,1)} %copy-done.2, ...), custom_call_target="tpu_custom_call" | custom-call | tf_op jit(solution)/shard_map/far/pallas_call | solution.py:341
Async XLA Ops:
  2.5 12.1 %collective-permute-start.1 = (bf16[32,32,128]{2,1,0:T(8,128)(2,1)}, bf16[32,32,128]{2,1,0:T(8,128)(2,1)S(1)}, u32[]{:S(2)}, u32[]{:S(2)}) collective-permute-start(bf16[32,32,128]{2,1,0:T(8,128)(2,1)} %get-tuple-element.12.own), channel_id=1, source_target_pairs={{1,2},{2,1},{3,4},{4,3},{5,6},{6,5},{7,8},{8,7},{9,10},{10,9},{11,... | collective-permute-start | bytes 786440 | tf_op jit(solution)/shard_map/ppermute | solution.py:309
  4.4 10.1 %collective-permute-start = (bf16[32,32,128]{2,1,0:T(8,128)(2,1)}, bf16[32,32,128]{2,1,0:T(8,128)(2,1)S(1)}, u32[]{:S(2)}, u32[]{:S(2)}) collective-permute-start(bf16[32,32,128]{2,1,0:T(8,128)(2,1)} %get-tuple-element.12.own), channel_id=1, source_target_pairs={{0,1},{1,0},{2,3},{3,2},{4,5},{5,4},{6,7},{7,6},{8,9},{9,8},{10,11... | collective-permute-start | bytes 786440 | tf_op jit(solution)/shard_map/ppermute | solution.py:308
  6.1 30.6 %all-to-all-start = ((bf16[64,32,128]{2,1,0:T(8,128)(2,1)}), bf16[64,32,128]{2,1,0:T(8,128)(2,1)S(1)}, u32[]{:S(2)}, u32[]{:S(2)}) async-start(bf16[64,32,128]{2,1,0:T(8,128)(2,1)} %get-tuple-element.16), calls=%async_computation | async-start | bytes 1048576 | tf_op jit(solution)/shard_map/all_to_all | solution.py:307
  14.6 0.7 %copy-start.1 = (bf16[32,32,128]{2,1,0:T(8,128)(2,1)}, bf16[32,32,128]{2,1,0:T(8,128)(2,1)S(1)}, u32[]{:S(2)}) copy-start(bf16[32,32,128]{2,1,0:T(8,128)(2,1)S(1)} %collective-permute-done.1.other) | copy-start | bytes 786436
  14.6 0.8 %copy-start.2 = (bf16[32,32,128]{2,1,0:T(8,128)(2,1)}, bf16[32,32,128]{2,1,0:T(8,128)(2,1)S(1)}, u32[]{:S(2)}) copy-start(bf16[32,32,128]{2,1,0:T(8,128)(2,1)S(1)} %collective-permute-done.twin) | copy-start | bytes 786436
  36.7 0.8 %copy-start = (bf16[64,32,128]{2,1,0:T(8,128)(2,1)}, bf16[64,32,128]{2,1,0:T(8,128)(2,1)S(1)}, u32[]{:S(2)}) copy-start(bf16[64,32,128]{2,1,0:T(8,128)(2,1)S(1)} %all-to-all-done.arrived_hbm) | copy-start | bytes 1572868

commit v3 on v2

v3 whole, which is shorter than its diff:
```python
import functools

import jax
import jax.numpy as jnp
from jax import lax
from jax.experimental import pallas as pl
from jax.experimental.pallas import tpu as pltpu
from jax.sharding import PartitionSpec as P

F32 = jnp.float32
BF16 = jnp.bfloat16
I32 = jnp.int32
VMEM = pl.BlockSpec(memory_space=pltpu.VMEM)
SMEM = pl.BlockSpec(memory_space=pltpu.SMEM)
HBM = pl.BlockSpec(memory_space=pltpu.HBM)
GROUP = 32
SLOTS = 16
FEW = 8
ITEMS = 24
LANES = 128
NT = (((1,), (1,)), ((), ()))


def params(mib):
    return pltpu.CompilerParams(vmem_limit_bytes=mib << 20)


def padded(n, m):
    return -(-n // m) * m


def pack_kernel(me, send, m_hbm, own_hbm, outgoing_hbm, m, ids, scr, own, outgoing, sems):
    batches, pairs = own.shape[0], own.shape[1]
    slots, devices = ids.shape
    rows = pltpu.make_async_copy(m_hbm, m, sems.at[0])
    lists = pltpu.make_async_copy(send.at[me[0]], ids, sems.at[1])
    rows.start()
    lists.start()
    rows.wait()
    for i in range(pairs):
        for h in range(0, batches, 16):
            x = m[h : h + 16, i * LANES : (i + 1) * LANES].astype(F32)
            scr[pl.ds(h * pairs + i, 16, stride=pairs), :] = x
    for b in range(batches):
        own[b] = scr[b * pairs : (b + 1) * pairs, :].astype(BF16)
    keep = pltpu.make_async_copy(own, own_hbm, sems.at[2])
    keep.start()
    lists.wait()
    first = me[0] * batches
    part = devices // 4
    done = []
    for c in range(4):

        def send_to(j, _):
            for k in range(slots):
                outgoing[j * slots + k] = own[ids[k, j] - first]
            return 0

        lax.fori_loop(c * part, (c + 1) * part, send_to, 0, unroll=8)
        here = pl.ds(c * part * slots, part * slots)
        done.append(pltpu.make_async_copy(outgoing.at[here], outgoing_hbm.at[here], sems.at[3 + c]))
        done[-1].start()
    keep.wait()
    for copy in done:
        copy.wait()


def turn_ops(native, ops):
    coeffs, offsets = native.shape[0], native.shape[2]
    half = coeffs // 2
    tall = ops.shape[0]
    at = lax.broadcasted_iota(I32, (tall, offsets), 0)
    eye = jnp.where(at == lax.broadcasted_iota(I32, (tall, offsets), 1), 1.0, 0.0).astype(BF16)
    for i in range(0, half, 16):
        blocks = []
        for c in range(i, i + 16, 8):
            found = []
            for k in range(c, c + 8, 2):
                x = jnp.concatenate([native[k], native[half + k], native[k + 1], native[half + k + 1]], axis=0)
                y = lax.dot_general(eye, x, NT, preferred_element_type=F32)
                found += [y[:, :LANES], y[:, LANES:]]
            blocks.append(jnp.swapaxes(jnp.stack(found, axis=0), 0, 1))
        ops[:, i : i + 16, :] = jnp.concatenate(blocks, axis=1).astype(BF16)


def swapped(x):
    half = x.shape[1] // 2
    return jnp.concatenate([x[:, half:], x[:, :half]], axis=1)


def one_hot(want, row):
    return jnp.where(want == row, 1.0, 0.0).astype(BF16)


def make_tables(total_batches, me, src, off, live, near_slots, late):
    rows, lst = src.shape
    slots, wide = SLOTS, near_slots.shape[0]
    s = src[...]
    o = off[...]
    mine = me[0] * rows
    twin = (me[0] ^ 1) * rows
    other = (me[0] - 1 + 2 * (me[0] & 1)) * rows
    at_r = lax.broadcasted_iota(I32, (rows, rows), 0)
    at_c = lax.broadcasted_iota(I32, (rows, rows), 1)
    count_col = jnp.sum(jnp.where(at_r == at_c, live[...], 0), axis=1, keepdims=True)
    alive = lax.broadcasted_iota(I32, (rows, lst), 1) < count_col
    far = s >= total_batches
    in_mine = (s >= mine) & (s < mine + rows)
    in_twin = (s >= twin) & (s < twin + rows)
    place = jnp.where(in_mine, s - mine, jnp.where(in_twin, s - twin + rows, s - other + 2 * rows))
    place = jnp.where(far, s - total_batches + 3 * rows, place)
    value = jnp.where(alive, place + 1, 0)
    both = jnp.concatenate([value & 127, value >> 7], axis=0).astype(F32).astype(BF16)
    want = lax.broadcasted_iota(I32, (wide, lst), 0)
    lows, highs = [], []
    for t in range(rows):
        got = lax.dot_general(both, one_hot(want, o[t : t + 1, :]), NT, preferred_element_type=F32)
        lows.append(got[t : t + 1, :])
        highs.append(got[rows + t : rows + t + 1, :])
    low = jnp.concatenate(lows, axis=0)
    high = jnp.concatenate(highs, axis=0)
    value = (low + 128.0 * high).astype(I32)
    near = (value > 0) & (value <= 3 * rows)
    sooner = jnp.where(at_c < at_r, 1.0, 0.0).astype(BF16)
    rank = jnp.dot(sooner, jnp.where(near, 1.0, 0.0).astype(BF16), preferred_element_type=F32).astype(I32)
    target = lax.broadcasted_iota(I32, (rows, wide), 0)
    sources, targets = [], []
    for r in range(slots):
        sel = near & (rank == r)
        sources.append(jnp.sum(jnp.where(sel, value, 0), axis=0, keepdims=True))
        targets.append(jnp.sum(jnp.where(sel, target - rows, 0), axis=0, keepdims=True) + rows)
    table = jnp.concatenate(sources + targets, axis=0).astype(F32)
    near_slots[:, 0 : 2 * slots] = table.T.astype(I32)
    behind = (value > 3 * rows) | (near & (rank >= slots))
    one = jnp.where(behind, 1.0, 0.0)
    before = lax.broadcasted_iota(I32, (wide, wide), 0) < lax.broadcasted_iota(I32, (wide, wide), 1)
    order = jnp.dot(one.astype(BF16), jnp.where(before, 1.0, 0.0).astype(BF16), preferred_element_type=F32)
    pos = jnp.where(behind, order.astype(I32), wide)
    count = jnp.sum(one, axis=1, keepdims=True).astype(I32)
    items = jnp.maximum((count + (FEW - 1)) // FEW, 1)
    late[:, 0:wide] = jnp.zeros((late.shape[0], wide), I32)
    late[:, wide:] = jnp.ones((late.shape[0], late.shape[1] - wide), I32)
    late[0:rows, wide:] = jnp.broadcast_to(items, (rows, late.shape[1] - wide))
    want = lax.broadcasted_iota(I32, (wide, wide), 0)
    offset = lax.broadcasted_iota(I32, (16, wide), 1).astype(F32)
    parts = jnp.concatenate([low, high, offset], axis=0).astype(BF16)
    for t in range(rows):
        got = lax.dot_general(parts, one_hot(want, pos[t : t + 1, :]), NT, preferred_element_type=F32).astype(I32)
        source = got[t : t + 1, :] + 128 * got[rows + t : rows + t + 1, :]
        late[t : t + 1, 0:wide] = source * 256 + got[2 * rows : 2 * rows + 1, :]


def near_kernel(
    total_batches, me, src_hbm, off_hbm, live_hbm, native_hbm, own, twin, other,
    sums, ops_hbm, late_hbm,
    src, off, live, native, ops, late, slots_v, slot_t, pool, acc_a, acc_b, acc_c, acc_d, sems,
):
    batches, pairs = own.shape[0], own.shape[1]
    lists = []
    for n, (x, y) in enumerate(((src_hbm, src), (off_hbm, off), (live_hbm, live))):
        lists.append(pltpu.make_async_copy(x, y, sems.at[n]))
    fetch = pltpu.make_async_copy(native_hbm, native, sems.at[3])
    parts = []
    for n, part in enumerate((own, twin, other)):
        parts.append(pltpu.make_async_copy(part, pool.at[pl.ds(1 + n * batches, batches)], sems.at[4 + n]))
    for copy in lists + [fetch] + parts:
        copy.start()
    pool[0] = jnp.zeros(pool.shape[1:], BF16)
    accs = (acc_a, acc_b, acc_c, acc_d)
    for acc in accs:
        acc[...] = jnp.zeros_like(acc)
    for copy in lists:
        copy.wait()
    make_tables(total_batches, me, src, off, live, slots_v, late)
    to_smem = pltpu.make_async_copy(slots_v, slot_t, sems.at[7])
    to_smem.start()
    keep_late = pltpu.make_async_copy(late, late_hbm, sems.at[0])
    keep_late.start()
    fetch.wait()
    turn_ops(native, ops)
    keep = pltpu.make_async_copy(ops, ops_hbm, sems.at[1])
    keep.start()
    for copy in parts:
        copy.wait()
    to_smem.wait()
    slots = SLOTS
    blank = jnp.zeros(ops.shape[1:], BF16)
    none = jnp.zeros((LANES, LANES), BF16)
    low = lax.broadcasted_iota(I32, blank.shape, 1) < LANES // 2

    def twice(l):
        x = ops[l]
        y = swapped(x)
        first = [jnp.where(low, x, blank), jnp.where(low, y, blank)]
        return jnp.concatenate(first + [jnp.where(low, blank, y), jnp.where(low, blank, x)], axis=0)

    def group(g, _):
        for h in range(0, GROUP, 2):
            l = g * GROUP + h
            top = jnp.concatenate([twice(l), none], axis=1)
            end = jnp.concatenate([none, twice(l + 1)], axis=1)
            w = jnp.concatenate([top, end], axis=0)
            rows = [jnp.concatenate([pool[slot_t[l, r]], pool[slot_t[l + 1, r]]], axis=1) for r in range(slots)]
            y = lax.dot_general(jnp.concatenate(rows, axis=0), w, NT, preferred_element_type=F32)
            for side in range(2):
                acc = accs[(h % 4) // 2 * 2 + side]
                for r in range(0, slots, 4):
                    ats = [slot_t[l + side, slots + r + k] for k in range(4)]
                    olds = [acc[at] for at in ats]
                    for k in range(4):
                        new = y[(r + k) * pairs : (r + k + 1) * pairs, side * LANES : (side + 1) * LANES]
                        acc[ats[k]] = olds[k] + new
        return 0

    lax.fori_loop(0, slot_t.shape[0] // GROUP, group, 0)

    part = batches // 4
    done = []
    for c in range(4):
        for t in range(c * part, (c + 1) * part):
            acc_a[t] = (acc_a[t] + acc_b[t]) + (acc_c[t] + acc_d[t])
        here = pl.ds(c * part, part)
        done.append(pltpu.make_async_copy(acc_a.at[here], sums.at[here], sems.at[2 + c]))
        done[-1].start()
    keep_late.wait()
    keep.wait()
    for copy in done:
        copy.wait()


def far_kernel(
    table_hbm, own, twin, other, ops_hbm, near_hbm, arrived_hbm, occ_hbm, out_hbm,
    table, blocks, ops, near, occ, pool, acc, out, sems,
):
    batches, pairs = near.shape[0], near.shape[1]
    many = arrived_hbm.shape[0]
    last = table.shape[1] - 1
    fetch_table = pltpu.make_async_copy(table_hbm, table, sems.at[0])
    fetch_ops = pltpu.make_async_copy(ops_hbm, ops, sems.at[1])
    fetch_near = pltpu.make_async_copy(near_hbm, near, sems.at[2])
    fetch_occ = pltpu.make_async_copy(occ_hbm, occ, sems.at[3])
    parts = []
    for n, part in enumerate((own, twin, other, arrived_hbm)):
        here = pl.ds(n * batches, part.shape[0])
        parts.append(pltpu.make_async_copy(part, blocks.at[here], sems.at[4 + n]))
    for copy in [fetch_table] + parts + [fetch_ops, fetch_near, fetch_occ]:
        copy.start()
    acc[...] = jnp.zeros_like(acc)
    pool[0] = jnp.zeros(pool.shape[1:], BF16)
    for copy in parts:
        copy.wait()

    def spread(source, target, start):
        def put(n, _):
            x = source[n]
            target[start + n, 0:pairs] = x
            target[start + n, pairs : 2 * pairs] = swapped(x)
            return 0

        lax.fori_loop(0, source.shape[0], put, 0, unroll=16)

    spread(blocks, pool, 1)
    fetch_table.wait()
    fetch_ops.wait()
    half = LANES // 2
    low = lax.broadcasted_iota(I32, (pairs, LANES), 1) < half
    total = lax.fori_loop(0, batches, lambda t, n: n + table[t, last], 0)

    def step(i, place):
        t, g = place
        for u in range(ITEMS):
            xs, ws = [], []
            for h in range(0, FEW, 2):
                e = g * FEW + h
                va, vb = table[t, e], table[t, e + 1]
                a, b = va >> 8, vb >> 8
                even = jnp.where(low, pool[a, 0:pairs], pool[b, pairs : 2 * pairs])
                odd = jnp.where(low, pool[a, pairs : 2 * pairs], pool[b, 0:pairs])
                xs.append(jnp.concatenate([even, odd], axis=0))
                wa, wb = ops[va & 255], ops[vb & 255]
                ws.append(jnp.concatenate([jnp.where(low, wa, swapped(wb)), jnp.where(low, swapped(wa), wb)], axis=0))
            r = lax.dot_general(jnp.concatenate(xs, axis=1), jnp.concatenate(ws, axis=1), NT, preferred_element_type=F32)
            at = pl.ds(pl.multiple_of(t * pairs, pairs), pairs)
            acc[at, :] += jnp.concatenate([r[:pairs], r[pairs:]], axis=1)
            end = g + 1 >= table[t, last]
            t = jnp.where(end, jnp.minimum(t + 1, batches), t)
            g = jnp.where(end, 0, g + 1)
        return t, g

    lax.fori_loop(0, (total + (ITEMS - 1)) // ITEMS, step, (jnp.int32(0), jnp.int32(0)))
    fetch_near.wait()
    fetch_occ.wait()

    def join(t, _):
        at = pl.ds(pl.multiple_of(t * pairs, pairs), pairs)
        acc[at, :] += near[t]
        return 0

    lax.fori_loop(0, batches, join, 0, unroll=8)
    cells = occ.shape[1]
    filled = occ[...].astype(F32).astype(BF16)
    cell = lax.broadcasted_iota(I32, (cells, LANES), 0)
    odd_cell = (lax.broadcasted_iota(I32, (cells, LANES), 1) >= half).astype(I32)
    done = []
    for i in range(pairs):
        spread = jnp.where(cell == odd_cell + 2 * i, 1.0, 0.0).astype(BF16)
        keep = jnp.dot(filled, spread, preferred_element_type=F32)
        out[:, i * LANES : (i + 1) * LANES] = acc[pl.ds(i, batches, stride=pairs), :] * keep
        if i % 8 == 7:
            here = pl.ds((i - 7) * LANES, 8 * LANES)
            done.append(pltpu.make_async_copy(out.at[:, here], out_hbm.at[:, here], sems.at[i // 8]))
            done[-1].start()
    for copy in done:
        copy.wait()


def local(multipoles, operators, pair_source, pair_offset, live_pairs, send_lists, occupied):
    axes = ("key", "lvl")
    batches, width = multipoles.shape
    offsets, coeffs = operators.shape[0], operators.shape[1]
    devices = lax.axis_size(axes)
    slots = send_lists.shape[2]
    me = lax.axis_index(axes)
    pairs = width // LANES
    wide = padded(offsets, GROUP)
    wide = padded(wide, 64)
    block = (pairs, LANES)

    own, outgoing = pl.pallas_call(
        pack_kernel,
        out_shape=(
            jax.ShapeDtypeStruct((batches,) + block, BF16),
            jax.ShapeDtypeStruct((devices * slots,) + block, BF16),
        ),
        in_specs=[SMEM, HBM, HBM],
        out_specs=(HBM, HBM),
        scratch_shapes=[
            pltpu.VMEM((batches, width), BF16),
            pltpu.SMEM((slots, devices), I32),
            pltpu.VMEM((batches * pairs, LANES), F32),
            pltpu.VMEM((batches,) + block, BF16),
            pltpu.VMEM((devices * slots,) + block, BF16),
            pltpu.SemaphoreType.DMA((7,)),
        ],
        compiler_params=params(56),
        name="pack",
    )(me.reshape(1), send_lists.transpose(0, 2, 1), multipoles)
    even = [(i, i ^ 1) for i in range(devices)]
    odd = [p for i in range(1, devices - 1, 2) for p in ((i, i + 1), (i + 1, i))]
    arrived = lax.all_to_all(outgoing, axes, split_axis=0, concat_axis=0, tiled=True)
    twin = lax.ppermute(own, axes, even)
    other = lax.ppermute(own, axes, odd)
    tall = padded(batches + 1, 8)
    ops_shape = (wide, coeffs // 2, LANES)
    late_shape = (tall, padded(wide + 1, LANES))
    sums, ops, late = pl.pallas_call(
        functools.partial(near_kernel, batches * devices),
        out_shape=(
            jax.ShapeDtypeStruct((batches,) + block, F32),
            jax.ShapeDtypeStruct(ops_shape, BF16),
            jax.ShapeDtypeStruct(late_shape, I32),
        ),
        in_specs=[SMEM] + [HBM] * 7,
        out_specs=(HBM,) * 3,
        scratch_shapes=[
            pltpu.VMEM((batches, offsets), I32),
            pltpu.VMEM((batches, offsets), I32),
            pltpu.VMEM((1, batches), I32),
            pltpu.VMEM((coeffs, coeffs, offsets), BF16),
            pltpu.VMEM(ops_shape, BF16),
            pltpu.VMEM(late_shape, I32),
            pltpu.VMEM((wide, LANES), I32),
            pltpu.SMEM((wide, LANES), I32),
            pltpu.VMEM((3 * batches + 1,) + block, BF16),
        ]
        + [pltpu.VMEM((batches + 1,) + block, F32)] * 4
        + [pltpu.SemaphoreType.DMA((8,))],
        compiler_params=params(56),
        cost_estimate=pl.CostEstimate(flops=12_000_000_000, bytes_accessed=4_000_000, transcendentals=0),
        name="near",
    )(me.reshape(1), pair_source, pair_offset, live_pairs.reshape(1, batches), operators.transpose(1, 2, 0), own, twin, other)

    many = 3 * batches + devices * slots
    return pl.pallas_call(
        far_kernel,
        out_shape=jax.ShapeDtypeStruct((batches, width), F32),
        in_specs=[HBM] * 8,
        out_specs=HBM,
        scratch_shapes=[
            pltpu.SMEM(late_shape, I32),
            pltpu.VMEM((many,) + block, BF16),
            pltpu.VMEM(ops_shape, BF16),
            pltpu.VMEM((batches,) + block, F32),
            pltpu.VMEM(occupied.shape, I32),
            pltpu.VMEM((many + 1, 2 * pairs, LANES), BF16),
            pltpu.VMEM(((batches + 1) * pairs, LANES), F32),
            pltpu.VMEM((batches, width), F32),
            pltpu.SemaphoreType.DMA((8,)),
        ],
        compiler_params=params(56),
        name="far",
    )(late, own, twin, other, ops, sums, arrived, occupied)


def solution(mesh):
    spec = P(("key", "lvl"), None)
    return jax.shard_map(
        local,
        mesh=mesh,
        in_specs=(spec, P(), spec, spec, P(("key", "lvl")), P(), spec),
        out_specs=spec,
        check_vma=False,
    )
```

time: 47.1 us -> 42.6 us (0.904)
  the two profiles are of different devices: /device:TPU:14 before, /device:TPU:6 now
where the time goes in v3:
time: 42.6 us; the launch traced here: 42.1 us
  Pallas kernels  28.6 us (67%)
  starting transfers between devices  8.72 us (20%)
  waiting for transfers between devices  3.08 us (7%)
  local copies, waits for them, and re-layouts  1.62 us (4%)
    pallas_call x1, Pallas kernels, local(): pl.pallas_call(functools.partial(near_kernel, batches * devices), out_sha...  17.8 us
    pallas_call x1, Pallas kernels, local(): pl.pallas_call(far_kernel, out_shape=jax.ShapeDtypeStruct((batches, width...  8.41 us
    all_to_all x1, starting transfers between devices, local(): lax.all_to_all(outgoing, axes, split_axis=0, concat_axis=0, tiled=True)  5.14 us
    ppermute x1, waiting for transfers between devices, local(): other = lax.ppermute(own, axes, odd)  3.07 us
    pallas_call x1, Pallas kernels, local(): pl.pallas_call(pack_kernel, out_shape=(jax.ShapeDtypeStruct((batches,) +...  2.39 us
    ppermute x1, starting transfers between devices, local(): other = lax.ppermute(own, axes, odd)  1.92 us
    ppermute x1, starting transfers between devices, local(): twin = lax.ppermute(own, axes, even)  1.66 us
    unnamed x6, local copies, waits for them, and re-layouts  1.62 us
  transfers between devices with their start and end apart: 3, of which 1 were waited for; matrix products, arithmetic and copies ran while one was open for 0% of the time, Pallas kernels for 42%

profile of v3, /device:TPU:6, one launch (start us, length us, event | category | flops | bytes accessed | tf_op | source)
XLA Modules:
  0.0 42.1 jit_solution(17980187202883111347)
XLA Ops:
  0.0 2.4 %pack.1 = (bf16[32,32,128]{2,1,0:T(8,128)(2,1)}, bf16[64,32,128]{2,1,0:T(8,128)(2,1)}) custom-call(s32[1]{0:T(128)} %bitcast.me, s32[32,2,32]{2,1,0:T(2,128)} %bitcast.4, bf16[32,4096]{1,0:T(8,128)(2,1)} %m_hbm.1), custom_call_target="tpu_custom_call" | custom-call | tf_op jit(solution)/shard_map/pack/pallas_call | solution.py:329
  2.4 1.9 %collective-permute-start.1 = (bf16[32,32,128]{2,1,0:T(8,128)(2,1)}, bf16[32,32,128]{2,1,0:T(8,128)(2,1)S(1)}, u32[]{:S(2)}, u32[]{:S(2)}) collective-permute-start(bf16[32,32,128]{2,1,0:T(8,128)(2,1)} %get-tuple-element.10.own), channel_id=1, source_target_pairs={{1,2},{2,1},{3,4},{4,3},{5,6},{6,5},{7,8},{8,7},{9,10},{10,9},{11,... | collective-permute-start | bytes 786440 | tf_op jit(solution)/shard_map/ppermute | solution.py:352
  4.3 1.7 %collective-permute-start = (bf16[32,32,128]{2,1,0:T(8,128)(2,1)}, bf16[32,32,128]{2,1,0:T(8,128)(2,1)S(1)}, u32[]{:S(2)}, u32[]{:S(2)}) collective-permute-start(bf16[32,32,128]{2,1,0:T(8,128)(2,1)} %get-tuple-element.10.own), channel_id=1, source_target_pairs={{0,1},{1,0},{2,3},{3,2},{4,5},{5,4},{6,7},{7,6},{8,9},{9,8},{10,11... | collective-permute-start | bytes 786440 | tf_op jit(solution)/shard_map/ppermute | solution.py:351
  6.0 5.1 %all-to-all-start = ((bf16[64,32,128]{2,1,0:T(8,128)(2,1)}), bf16[64,32,128]{2,1,0:T(8,128)(2,1)S(1)}, u32[]{:S(2)}, u32[]{:S(2)}) async-start(bf16[64,32,128]{2,1,0:T(8,128)(2,1)} %get-tuple-element.14), calls=%async_computation | async-start | bytes 1048576 | tf_op jit(solution)/shard_map/all_to_all | solution.py:350
  11.1 3.1 %collective-permute-done.1.other = bf16[32,32,128]{2,1,0:T(8,128)(2,1)S(1)} collective-permute-done((bf16[32,32,128]{2,1,0:T(8,128)(2,1)}, bf16[32,32,128]{2,1,0:T(8,128)(2,1)S(1)}, u32[]{:S(2)}, u32[]{:S(2)}) %collective-permute-start.1) | collective-permute-done | bytes 262176 | tf_op jit(solution)/shard_map/ppermute | solution.py:352
  14.2 0.0 copy-start.1
  14.2 0.0 collective-permute-done.twin
  14.2 0.0 copy-start.2
  14.2 0.7 %copy-done.1 = bf16[32,32,128]{2,1,0:T(8,128)(2,1)} copy-done((bf16[32,32,128]{2,1,0:T(8,128)(2,1)}, bf16[32,32,128]{2,1,0:T(8,128)(2,1)S(1)}, u32[]{:S(2)}) %copy-start.1) | copy-done | bytes 262168
  14.9 0.1 copy-done.2
  15.0 17.8 %near.1 = (f32[32,32,128]{2,1,0:T(8,128)}, bf16[192,32,128]{2,1,0:T(8,128)(2,1)}, s32[40,256]{1,0:T(8,128)}) custom-call(s32[1]{0:T(128)} %bitcast.me, s32[32,189]{1,0:T(8,128)} %src_hbm.1, s32[32,189]{1,0:T(8,128)} %off_hbm.1, s32[1,32]{1,0:T(1,128)} %bitcast.6, bf16[64,64,189]{2,1,0:T(8,128)(2,1)} %bitcast.5, bf16[32,32,128]{2,1,0:T(8,128)(2,1)} %get-tuple-element.10.own, ...), custom_call_target="tpu_custom_call" | custom-call | flops 12000000000 | bytes 4000000 | tf_op jit(solution)/shard_map/near/pallas_call | solution.py:356
  32.8 0.0 all-to-all-done.arrived_hbm
  32.9 0.0 copy-start
  32.9 0.8 %copy-done = bf16[64,32,128]{2,1,0:T(8,128)(2,1)} copy-done((bf16[64,32,128]{2,1,0:T(8,128)(2,1)}, bf16[64,32,128]{2,1,0:T(8,128)(2,1)S(1)}, u32[]{:S(2)}) %copy-start) | copy-done | bytes 524312
  33.7 8.4 %far.1 = f32[32,4096]{1,0:T(8,128)} custom-call(s32[40,256]{1,0:T(8,128)} %get-tuple-element.11.table_hbm, bf16[32,32,128]{2,1,0:T(8,128)(2,1)} %get-tuple-element.10.own, bf16[32,32,128]{2,1,0:T(8,128)(2,1)} %copy-done.2, bf16[32,32,128]{2,1,0:T(8,128)(2,1)} %copy-done.1, bf16[192,32,128]{2,1,0:T(8,128)(2,1)} %get-tuple-element.12.ops_hbm, ...), custom_call_target="tpu_custom_call" | custom-call | tf_op jit(solution)/shard_map/far/pallas_call | solution.py:384
Async XLA Ops:
  2.4 11.8 %collective-permute-start.1 = (bf16[32,32,128]{2,1,0:T(8,128)(2,1)}, bf16[32,32,128]{2,1,0:T(8,128)(2,1)S(1)}, u32[]{:S(2)}, u32[]{:S(2)}) collective-permute-start(bf16[32,32,128]{2,1,0:T(8,128)(2,1)} %get-tuple-element.10.own), channel_id=1, source_target_pairs={{1,2},{2,1},{3,4},{4,3},{5,6},{6,5},{7,8},{8,7},{9,10},{10,9},{11,... | collective-permute-start | bytes 786440 | tf_op jit(solution)/shard_map/ppermute | solution.py:352
  4.3 9.9 %collective-permute-start = (bf16[32,32,128]{2,1,0:T(8,128)(2,1)}, bf16[32,32,128]{2,1,0:T(8,128)(2,1)S(1)}, u32[]{:S(2)}, u32[]{:S(2)}) collective-permute-start(bf16[32,32,128]{2,1,0:T(8,128)(2,1)} %get-tuple-element.10.own), channel_id=1, source_target_pairs={{0,1},{1,0},{2,3},{3,2},{4,5},{5,4},{6,7},{7,6},{8,9},{9,8},{10,11... | collective-permute-start | bytes 786440 | tf_op jit(solution)/shard_map/ppermute | solution.py:351
  6.0 26.9 %all-to-all-start = ((bf16[64,32,128]{2,1,0:T(8,128)(2,1)}), bf16[64,32,128]{2,1,0:T(8,128)(2,1)S(1)}, u32[]{:S(2)}, u32[]{:S(2)}) async-start(bf16[64,32,128]{2,1,0:T(8,128)(2,1)} %get-tuple-element.14), calls=%async_computation | async-start | bytes 1048576 | tf_op jit(solution)/shard_map/all_to_all | solution.py:350
  14.2 0.7 %copy-start.1 = (bf16[32,32,128]{2,1,0:T(8,128)(2,1)}, bf16[32,32,128]{2,1,0:T(8,128)(2,1)S(1)}, u32[]{:S(2)}) copy-start(bf16[32,32,128]{2,1,0:T(8,128)(2,1)S(1)} %collective-permute-done.1.other) | copy-start | bytes 786436
  14.2 0.8 %copy-start.2 = (bf16[32,32,128]{2,1,0:T(8,128)(2,1)}, bf16[32,32,128]{2,1,0:T(8,128)(2,1)S(1)}, u32[]{:S(2)}) copy-start(bf16[32,32,128]{2,1,0:T(8,128)(2,1)S(1)} %collective-permute-done.twin) | copy-start | bytes 786436
  32.9 0.8 %copy-start = (bf16[64,32,128]{2,1,0:T(8,128)(2,1)}, bf16[64,32,128]{2,1,0:T(8,128)(2,1)S(1)}, u32[]{:S(2)}) copy-start(bf16[64,32,128]{2,1,0:T(8,128)(2,1)S(1)} %all-to-all-done.arrived_hbm) | copy-start | bytes 1572868

commit v4 on v3

--- a/solution.py
+++ b/solution.py
@@ -13,10 +13,10 @@
 VMEM = pl.BlockSpec(memory_space=pltpu.VMEM)
 SMEM = pl.BlockSpec(memory_space=pltpu.SMEM)
 HBM = pl.BlockSpec(memory_space=pltpu.HBM)
-GROUP = 32
+GROUP = 64
 SLOTS = 16
-FEW = 8
-ITEMS = 24
+FEW = 4
+ITEMS = 32
 LANES = 128
 NT = (((1,), (1,)), ((), ()))
 
@@ -247,19 +247,16 @@
         copy.start()
     acc[...] = jnp.zeros_like(acc)
     pool[0] = jnp.zeros(pool.shape[1:], BF16)
-    for copy in parts:
-        copy.wait()
-
-    def spread(source, target, start):
-        def put(n, _):
-            x = source[n]
-            target[start + n, 0:pairs] = x
-            target[start + n, pairs : 2 * pairs] = swapped(x)
-            return 0
-
-        lax.fori_loop(0, source.shape[0], put, 0, unroll=16)
-
-    spread(blocks, pool, 1)
+
+    def put(n, _):
+        x = blocks[n]
+        pool[1 + n, 0:pairs] = x
+        pool[1 + n, pairs : 2 * pairs] = swapped(x)
+        return 0
+
+    for n, copy in enumerate(parts):
+        copy.wait()
+        lax.fori_loop(n * batches, n * batches + (batches if n < 3 else many), put, 0, unroll=16)
     fetch_table.wait()
     fetch_ops.wait()
     half = LANES // 2

time: 42.6 us -> 40.9 us (0.960)
  the two profiles are of different devices: /device:TPU:6 before, /device:TPU:28 now
where the time goes in v4:
time: 40.9 us; the launch traced here: 40.4 us
  Pallas kernels  28 us (68%)
  starting transfers between devices  8.5 us (21%)
  waiting for transfers between devices  2.2 us (5%)
  local copies, waits for them, and re-layouts  1.62 us (4%)
    pallas_call x1, Pallas kernels, local(): pl.pallas_call(functools.partial(near_kernel, batches * devices), out_sha...  17.4 us
    pallas_call x1, Pallas kernels, local(): pl.pallas_call(far_kernel, out_shape=jax.ShapeDtypeStruct((batches, width...  8.22 us
    all_to_all x1, starting transfers between devices, local(): lax.all_to_all(outgoing, axes, split_axis=0, concat_axis=0, tiled=True)  4.97 us
    pallas_call x1, Pallas kernels, local(): pl.pallas_call(pack_kernel, out_shape=(jax.ShapeDtypeStruct((batches,) +...  2.39 us
    ppermute x1, waiting for transfers between devices, local(): other = lax.ppermute(own, axes, odd)  2.2 us
    ppermute x1, starting transfers between devices, local(): other = lax.ppermute(own, axes, odd)  1.92 us
    unnamed x6, local copies, waits for them, and re-layouts  1.62 us
    ppermute x1, starting transfers between devices, local(): twin = lax.ppermute(own, axes, even)  1.6 us
  transfers between devices with their start and end apart: 3, of which 1 were waited for; matrix products, arithmetic and copies ran while one was open for 0% of the time, Pallas kernels for 43%

profile of v4, /device:TPU:28, one launch (start us, length us, event | category | flops | bytes accessed | tf_op | source)
XLA Modules:
  0.0 40.4 jit_solution(1964765501092652886)
XLA Ops:
  0.0 2.4 %pack.1 = (bf16[32,32,128]{2,1,0:T(8,128)(2,1)}, bf16[64,32,128]{2,1,0:T(8,128)(2,1)}) custom-call(s32[1]{0:T(128)} %bitcast.me, s32[32,2,32]{2,1,0:T(2,128)} %bitcast.4, bf16[32,4096]{1,0:T(8,128)(2,1)} %m_hbm.1), custom_call_target="tpu_custom_call" | custom-call | tf_op jit(solution)/shard_map/pack/pallas_call | solution.py:326
  2.4 1.9 %collective-permute-start.1 = (bf16[32,32,128]{2,1,0:T(8,128)(2,1)}, bf16[32,32,128]{2,1,0:T(8,128)(2,1)S(1)}, u32[]{:S(2)}, u32[]{:S(2)}) collective-permute-start(bf16[32,32,128]{2,1,0:T(8,128)(2,1)} %get-tuple-element.10.own), channel_id=1, source_target_pairs={{1,2},{2,1},{3,4},{4,3},{5,6},{6,5},{7,8},{8,7},{9,10},{10,9},{11,... | collective-permute-start | bytes 786440 | tf_op jit(solution)/shard_map/ppermute | solution.py:349
  4.3 1.6 %collective-permute-start = (bf16[32,32,128]{2,1,0:T(8,128)(2,1)}, bf16[32,32,128]{2,1,0:T(8,128)(2,1)S(1)}, u32[]{:S(2)}, u32[]{:S(2)}) collective-permute-start(bf16[32,32,128]{2,1,0:T(8,128)(2,1)} %get-tuple-element.10.own), channel_id=1, source_target_pairs={{0,1},{1,0},{2,3},{3,2},{4,5},{5,4},{6,7},{7,6},{8,9},{9,8},{10,11... | collective-permute-start | bytes 786440 | tf_op jit(solution)/shard_map/ppermute | solution.py:348
  5.9 5.0 %all-to-all-start = ((bf16[64,32,128]{2,1,0:T(8,128)(2,1)}), bf16[64,32,128]{2,1,0:T(8,128)(2,1)S(1)}, u32[]{:S(2)}, u32[]{:S(2)}) async-start(bf16[64,32,128]{2,1,0:T(8,128)(2,1)} %get-tuple-element.14), calls=%async_computation | async-start | bytes 1048576 | tf_op jit(solution)/shard_map/all_to_all | solution.py:347
  10.9 2.2 %collective-permute-done.1.other = bf16[32,32,128]{2,1,0:T(8,128)(2,1)S(1)} collective-permute-done((bf16[32,32,128]{2,1,0:T(8,128)(2,1)}, bf16[32,32,128]{2,1,0:T(8,128)(2,1)S(1)}, u32[]{:S(2)}, u32[]{:S(2)}) %collective-permute-start.1) | collective-permute-done | bytes 262176 | tf_op jit(solution)/shard_map/ppermute | solution.py:349
  13.1 0.0 copy-start.1
  13.1 0.0 collective-permute-done.twin
  13.1 0.0 copy-start.2
  13.1 0.7 %copy-done.1 = bf16[32,32,128]{2,1,0:T(8,128)(2,1)} copy-done((bf16[32,32,128]{2,1,0:T(8,128)(2,1)}, bf16[32,32,128]{2,1,0:T(8,128)(2,1)S(1)}, u32[]{:S(2)}) %copy-start.1) | copy-done | bytes 262168
  13.8 0.1 copy-done.2
  13.9 17.4 %near.1 = (f32[32,32,128]{2,1,0:T(8,128)}, bf16[192,32,128]{2,1,0:T(8,128)(2,1)}, s32[40,256]{1,0:T(8,128)}) custom-call(s32[1]{0:T(128)} %bitcast.me, s32[32,189]{1,0:T(8,128)} %src_hbm.1, s32[32,189]{1,0:T(8,128)} %off_hbm.1, s32[1,32]{1,0:T(1,128)} %bitcast.6, bf16[64,64,189]{2,1,0:T(8,128)(2,1)} %bitcast.5, bf16[32,32,128]{2,1,0:T(8,128)(2,1)} %get-tuple-element.10.own, ...), custom_call_target="tpu_custom_call" | custom-call | flops 12000000000 | bytes 4000000 | tf_op jit(solution)/shard_map/near/pallas_call | solution.py:353
  31.4 0.0 all-to-all-done.arrived_hbm
  31.4 0.0 copy-start
  31.4 0.8 %copy-done = bf16[64,32,128]{2,1,0:T(8,128)(2,1)} copy-done((bf16[64,32,128]{2,1,0:T(8,128)(2,1)}, bf16[64,32,128]{2,1,0:T(8,128)(2,1)S(1)}, u32[]{:S(2)}) %copy-start) | copy-done | bytes 524312
  32.2 8.2 %far.1 = f32[32,4096]{1,0:T(8,128)} custom-call(s32[40,256]{1,0:T(8,128)} %get-tuple-element.11.table_hbm, bf16[32,32,128]{2,1,0:T(8,128)(2,1)} %get-tuple-element.10.own, bf16[32,32,128]{2,1,0:T(8,128)(2,1)} %copy-done.2, bf16[32,32,128]{2,1,0:T(8,128)(2,1)} %copy-done.1, bf16[192,32,128]{2,1,0:T(8,128)(2,1)} %get-tuple-element.12.ops_hbm, ...), custom_call_target="tpu_custom_call" | custom-call | tf_op jit(solution)/shard_map/far/pallas_call | solution.py:381
Async XLA Ops:
  2.4 10.7 %collective-permute-start.1 = (bf16[32,32,128]{2,1,0:T(8,128)(2,1)}, bf16[32,32,128]{2,1,0:T(8,128)(2,1)S(1)}, u32[]{:S(2)}, u32[]{:S(2)}) collective-permute-start(bf16[32,32,128]{2,1,0:T(8,128)(2,1)} %get-tuple-element.10.own), channel_id=1, source_target_pairs={{1,2},{2,1},{3,4},{4,3},{5,6},{6,5},{7,8},{8,7},{9,10},{10,9},{11,... | collective-permute-start | bytes 786440 | tf_op jit(solution)/shard_map/ppermute | solution.py:349
  4.3 8.8 %collective-permute-start = (bf16[32,32,128]{2,1,0:T(8,128)(2,1)}, bf16[32,32,128]{2,1,0:T(8,128)(2,1)S(1)}, u32[]{:S(2)}, u32[]{:S(2)}) collective-permute-start(bf16[32,32,128]{2,1,0:T(8,128)(2,1)} %get-tuple-element.10.own), channel_id=1, source_target_pairs={{0,1},{1,0},{2,3},{3,2},{4,5},{5,4},{6,7},{7,6},{8,9},{9,8},{10,11... | collective-permute-start | bytes 786440 | tf_op jit(solution)/shard_map/ppermute | solution.py:348
  5.9 25.4 %all-to-all-start = ((bf16[64,32,128]{2,1,0:T(8,128)(2,1)}), bf16[64,32,128]{2,1,0:T(8,128)(2,1)S(1)}, u32[]{:S(2)}, u32[]{:S(2)}) async-start(bf16[64,32,128]{2,1,0:T(8,128)(2,1)} %get-tuple-element.14), calls=%async_computation | async-start | bytes 1048576 | tf_op jit(solution)/shard_map/all_to_all | solution.py:347
  13.1 0.7 %copy-start.1 = (bf16[32,32,128]{2,1,0:T(8,128)(2,1)}, bf16[32,32,128]{2,1,0:T(8,128)(2,1)S(1)}, u32[]{:S(2)}) copy-start(bf16[32,32,128]{2,1,0:T(8,128)(2,1)S(1)} %collective-permute-done.1.other) | copy-start | bytes 786436
  13.1 0.8 %copy-start.2 = (bf16[32,32,128]{2,1,0:T(8,128)(2,1)}, bf16[32,32,128]{2,1,0:T(8,128)(2,1)S(1)}, u32[]{:S(2)}) copy-start(bf16[32,32,128]{2,1,0:T(8,128)(2,1)S(1)} %collective-permute-done.twin) | copy-start | bytes 786436
  31.4 0.8 %copy-start = (bf16[64,32,128]{2,1,0:T(8,128)(2,1)}, bf16[64,32,128]{2,1,0:T(8,128)(2,1)S(1)}, u32[]{:S(2)}) copy-start(bf16[64,32,128]{2,1,0:T(8,128)(2,1)S(1)} %all-to-all-done.arrived_hbm) | copy-start | bytes 1572868
